TPU v7x, 32 devices: a whole 2x2x4 slice. The times are simulated.
32 devices in a mesh: gx: 2 (over y), gz: 16 (over z, x, core).
Axes of the slice: x: 2, y: 2, z: 4, core: 2. Of those that a mesh axis runs over, the one named last changes fastest.
Arguments:
- state: float32 [5, 4, 64, 512], P(None, 'gx', 'gz'), may hold values from -21 to 21
- cotangent: float32 [5, 4, 64, 512], P(None, 'gx', 'gz'), may hold values from -6 to 6
- local_inverse: float32 [64, 4, 64, 512], P(None, 'gx', 'gz'), may hold values from -0.25 to 1.7
- wall_tags: int32 [2, 4, 64], P(None, 'gx', 'gz'), may hold values 0 or 1
- w_in: float32 [5, 256], replicated, may hold values from -2.5 to 2.5
- b_in: float32 [256], replicated, may hold values from -3 to 3
- w_mid: bfloat16 [256, 256], replicated, may hold values from -0.375 to 0.375
- b_mid: float32 [256], replicated, may hold values from -3 to 3
- w_out: bfloat16 [256, 5], replicated, may hold values from -1.5 to 1.5
Outputs:
- grad_state: float32 [5, 4, 64, 512], P(None, 'gx', 'gz')
- grad_w_in: float32 [5, 256], replicated
- grad_b_in: float32 [256], replicated
- grad_w_mid: float32 [256, 256], replicated
- grad_b_mid: float32 [256], replicated
- grad_w_out: float32 [256, 5], replicated
All inputs are finite; a program needn't handle non-finite values. No bound on the sum of `wall_tags` on one device may be relied on, other than what follows from the above.
Results may differ from a plain program's by a relative error of at most 0.0085.
Values sent between devices are 32-bit elements; how exact they have to be, the bound alone decides.
A program may use at most 64 MiB of HBM per device.

v0:
```python
import math

import jax
import jax.numpy as jnp
from jax import lax
from jax.sharding import PartitionSpec as P

KAPPA = 0.5
DT_STEP = 0.5
EPS = 1e-06
precise = lax.Precision.HIGHEST


def extended(cells, sides, width):
    for axis, dim in sides:
        count = lax.axis_size(axis)
        head = lax.slice_in_dim(cells, 0, width, axis=dim)
        tail = lax.slice_in_dim(cells, cells.shape[dim] - width, cells.shape[dim], axis=dim)
        cells = jnp.concatenate(
            [
                lax.ppermute(tail, axis, [(i, (i + 1) % count) for i in range(count)]),
                cells,
                lax.ppermute(head, axis, [((i + 1) % count, i) for i in range(count)]),
            ],
            axis=dim,
        )
    return cells


def silu_slope(pre_act):
    sigmoid_value = jax.nn.sigmoid(pre_act)
    return sigmoid_value * (1.0 + pre_act * (1.0 - sigmoid_value))


def inner_rows(first_op, second_op, precision=None):
    return lax.dot_general(
        first_op,
        second_op,
        (((1,), (1,)), ((), ())),
        precision=precision,
        preferred_element_type=jnp.float32,
    )


def inner_first(first_op, second_op, precision=None):
    return lax.dot_general(
        first_op,
        second_op,
        (((0,), (0,)), ((), ())),
        precision=precision,
        preferred_element_type=jnp.float32,
    )


def face_terms(blocks_view, lower_nb, upper_nb, face_axis):
    lower_term = 0.5 * (lower_nb - jnp.take(blocks_view, 0, axis=face_axis))
    upper_term = 0.5 * (upper_nb - jnp.take(blocks_view, 3, axis=face_axis))
    zero_face = jnp.zeros_like(lower_term)
    return jnp.stack([lower_term, zero_face, zero_face, upper_term], axis=face_axis)


def coupling(blocks_view, lower_x, upper_x, lower_z, upper_z, wall_tags):
    bottom = (1.0 - 2.0 * wall_tags[0].astype(jnp.float32))[None, :, :, None, None, None]
    top_side = (1.0 - 2.0 * wall_tags[1].astype(jnp.float32))[None, :, :, None, None, None]
    lower_y = jnp.concatenate(
        [bottom * blocks_view[:, :, :, :1, :, 0, :], blocks_view[:, :, :, :-1, :, 3, :]], axis=3
    )
    upper_y = jnp.concatenate(
        [blocks_view[:, :, :, 1:, :, 0, :], top_side * blocks_view[:, :, :, -1:, :, 3, :]], axis=3
    )
    return (
        face_terms(blocks_view, lower_x, upper_x, 4)
        + face_terms(blocks_view, lower_y, upper_y, 5)
        + face_terms(blocks_view, lower_z, upper_z, 6)
    )


def per_device(state, cotangent, local_inverse, wall_tags, w_in, b_in, w_mid, b_mid, w_out):
    channels, x_elems, z_elems, line_nodes = state.shape
    y_elems = line_nodes // 64
    node_rows = x_elems * z_elems * line_nodes
    entry_count = channels * node_rows * lax.axis_size("gx") * lax.axis_size("gz")
    sum_squares = lax.psum(jnp.sum(state * state), ("gx", "gz"))
    inv_norm = lax.rsqrt(sum_squares / entry_count + EPS)
    adjoint = jnp.einsum(
        "nikjm,cikjn->cikjm",
        local_inverse.reshape(64, x_elems, z_elems, y_elems, 64),
        cotangent.reshape(channels, x_elems, z_elems, y_elems, 64),
        precision=precise,
    )
    adjoint_flat = adjoint.reshape(channels, x_elems, z_elems, line_nodes)
    blocks_view = adjoint.reshape(channels, x_elems, z_elems, y_elems, 4, 4, 4)
    x_send = jnp.concatenate([blocks_view[:, :-1, :, :, 0], blocks_view[:, -1:, :, :, 3]], axis=1)
    x_rims = extended(x_send, (("gx", 1),), 1)
    lower_x = jnp.concatenate([x_rims[:, :1], blocks_view[:, :-1, :, :, 3]], axis=1)
    upper_x = jnp.concatenate([blocks_view[:, 1:, :, :, 0], x_rims[:, -1:]], axis=1)
    z_send = jnp.concatenate(
        [blocks_view[:, :, :-1, :, :, :, 0], blocks_view[:, :, -1:, :, :, :, 3]], axis=2
    )
    z_rims = extended(z_send, (("gz", 2),), 1)
    lower_z = jnp.concatenate([z_rims[:, :, :1], blocks_view[:, :, :-1, :, :, :, 3]], axis=2)
    upper_z = jnp.concatenate([blocks_view[:, :, 1:, :, :, :, 0], z_rims[:, :, -1:]], axis=2)
    coupled = coupling(blocks_view, lower_x, upper_x, lower_z, upper_z, wall_tags).reshape(
        channels, x_elems, z_elems, line_nodes
    )
    state_rows = state.reshape(channels, node_rows)
    scaled_rows = inv_norm * state_rows
    pre_first = inner_first(w_in, scaled_rows, precise) + b_in[:, None]
    hidden_one = jax.nn.silu(pre_first).astype(jnp.bfloat16)
    pre_second = inner_first(w_mid, hidden_one) + b_mid[:, None]
    hidden_two = jax.nn.silu(pre_second).astype(jnp.bfloat16)
    out_grad = (DT_STEP * adjoint_flat.reshape(channels, node_rows)).astype(jnp.bfloat16)
    grad_out = inner_rows(hidden_two, out_grad)
    back_two = jnp.dot(w_out, out_grad, preferred_element_type=jnp.float32)
    delta_two = (back_two * silu_slope(pre_second)).astype(jnp.bfloat16)
    grad_mid = inner_rows(hidden_one, delta_two)
    grad_bmid = jnp.sum(delta_two, axis=1, dtype=jnp.float32)
    back_one = jnp.dot(w_mid, delta_two, preferred_element_type=jnp.float32)
    delta_one = back_one * silu_slope(pre_first)
    grad_in = inner_rows(scaled_rows, delta_one, precise)
    grad_bin = jnp.sum(delta_one, axis=1)
    back_input = jnp.dot(w_in, delta_one, precision=precise, preferred_element_type=jnp.float32)
    grad_state = (
        adjoint_flat
        + KAPPA * coupled
        + inv_norm * back_input.reshape(channels, x_elems, z_elems, line_nodes)
    )
    summed = lax.psum((grad_in, grad_bin, grad_mid, grad_bmid, grad_out), ("gx", "gz"))
    factor = 4.0 / math.sqrt(entry_count // channels)
    return (
        grad_state,
        summed[0] * factor,
        summed[1] * factor,
        summed[2] * factor,
        summed[3] * factor,
        summed[4] * factor,
    )


def solution(mesh):
    placed = (
        P(None, "gx", "gz", None),
        P(None, "gx", "gz", None),
        P(None, "gx", "gz", None),
        P(None, "gx", "gz"),
        P(),
        P(),
        P(),
        P(),
        P(),
    )
    return jax.shard_map(
        per_device,
        mesh=mesh,
        in_specs=placed,
        out_specs=(P(None, "gx", "gz", None), P(), P(), P(), P(), P()),
        check_vma=False,
    )
```

profile of v0, /device:TPU:0, one launch (start us, length us, event | category | flops | bytes accessed | tf_op | source)
XLA Modules:
  0.0 213.1 jit_solution(1044381306770788096)
XLA Ops:
  8.3 1.8 reshape.102
  10.1 2.9 %fusion.8 = f32[2,4,8,5,64]{4,3,2,1,0:T(8,128)S(1)} fusion(f32[64,2,4,8,64]{4,3,2,1,0:T(8,128)S(1)} %reshape.102, f32[5,2,4,8,64]{4,3,2,1,0:T(8,128)S(1)} %reshape.101), kind=kOutput, calls=%fused_computation.19 | convolution fusion | flops 15728640 | bytes 1212416 | tf_op jit(solution)/shard_map/nikjm,cikjn->cikjm/dot_general | solution.py:85
  15.5 2.5 %collective-permute-start = (f32[5,1,4,8,4,4]{3,5,4,2,1,0:T(4,128)}, f32[5,1,4,8,4,4]{3,5,4,2,1,0:T(4,128)}, u32[]{:S(2)}, u32[]{:S(2)}) collective-permute-start(f32[5,1,4,8,4,4]{3,5,4,2,1,0:T(4,128)} %get-tuple-element.97), channel_id=1, source_target_pairs={{0,16},{16,0},{1,17},{17,1},{2,18},{18,2},{3,19},{19,3},{4,20},{20... | collective-permute-start | bytes 30728 | tf_op jit(solution)/shard_map/ppermute | solution.py:21
  20.1 4.2 %collective-permute-start.3 = (f32[5,2,1,8,4,4]{3,5,4,2,1,0:T(4,128)}, f32[5,2,1,8,4,4]{3,5,4,2,1,0:T(4,128)}, u32[]{:S(2)}, u32[]{:S(2)}) collective-permute-start(f32[5,2,1,8,4,4]{3,5,4,2,1,0:T(4,128)} %slice.191), channel_id=1, source_target_pairs={{1,0},{2,1},{3,2},{4,3},{5,4},{6,5},{7,6},{8,7},{9,8},{10,9},{11,1... | collective-permute-start | bytes 15368 | tf_op jit(solution)/shard_map/ppermute | solution.py:23
  25.6 38.4 %psum.42 = f32[]{:T(128)} all-reduce(f32[]{:T(128)} %multiply_reduce_fusion), channel_id=1, replica_groups=mesh['gx'=2,'gz'=16] {'gx','gz'}, use_global_device_ids=true, to_apply=%region_1.8 | all-reduce | flops 1 | bytes 8 | tf_op jit(solution)/shard_map/psum | solution.py:83
  64.9 5.7 %multiply_convert_fusion.1 = (bf16[256,4096]{0,1:T(8,128)(2,1)S(1)}, f32[256,4096]{0,1:T(8,128)}) fusion(f32[256]{0:T(256)S(1)} %copy-done.9, f32[5,4096]{1,0:T(8,128)S(1)} %mul.176, f32[5,256]{1,0:T(8,128)S(1)} %copy-done.5), kind=kOutput, calls=%fused_computation.14 | convolution fusion | flops 69206016 | bytes 6379520 | tf_op jit(solution)/shard_map/dot_general | solution.py:46
  71.3 2.0 copy-done.2
  73.3 2.4 %convert_reduce_fusion = (f32[256]{0:T(256)}, bf16[256,4096]{0,1:T(8,128)(2,1)S(1)}) fusion(f32[256,4096]{0,1:T(8,128)S(1)} %fusion.1, bf16[5,4096]{1,0:T(8,128)(2,1)S(1)} %convert_element_type.37, bf16[256,5]{0,1:T(8,128)(2,1)S(1)} %copy-done.8), kind=kOutput, calls=%fused_computation.12 | convolution fusion | flops 22019840 | bytes 6336000 | tf_op jit(solution)/shard_map/dot_general | solution.py:114
  80.5 3.5 %fusion.10 = f32[256,5]{0,1:T(8,128)S(1)} fusion(bf16[5,4096]{1,0:T(8,128)(2,1)S(1)} %convert_element_type.37, f32[256,4096]{0,1:T(8,128)} %copy-done.2), kind=kOutput, calls=%fused_computation.21 | convolution fusion | flops 15728640 | bytes 4240384 | tf_op jit(solution)/shard_map/dot_general | solution.py:36
  84.6 2.4 %fusion.32 = (f32[256]{0:T(256)}, f32[256,4096]{0,1:T(8,128)S(1)}) fusion(f32[256,4096]{0,1:T(8,128)S(1)} %copy-done.12, bf16[256,4096]{0,1:T(8,128)(2,1)S(1)} %copy-done.11, bf16[256,256]{1,0:T(8,128)(2,1)S(1)} %copy-done), kind=kOutput, calls=%fused_computation.69 | convolution fusion | flops 546307840 | bytes 10617856 | tf_op jit(solution)/shard_map/dot_general | solution.py:118
  87.0 1.7 fusion.33
  88.7 3.6 %fusion.5 = f32[5,4096]{1,0:T(8,128)S(1)} fusion(f32[256,4096]{0,1:T(8,128)S(1)} %get-tuple-element.106, f32[5,256]{1,0:T(8,128)S(1)} %copy-done.5, f32[]{:T(128)S(6)} %rsqrt.3), kind=kOutput, calls=%fused_computation.10 | convolution fusion | flops 62935040 | bytes 4281348 | tf_op jit(solution)/shard_map/dot_general | solution.py:122
  96.4 1.9 copy.107
  98.3 42.5 %all-reduce = (f32[5,256]{1,0:T(8,128)S(1)}, f32[256]{0:T(256)}, f32[256]{0:T(256)}, f32[256,5]{0,1:T(8,128)S(1)}) all-reduce(f32[5,256]{1,0:T(8,128)S(1)} %fusion.33, f32[256]{0:T(256)} %get-tuple-element.105, f32[256]{0:T(256)} %get-tuple-element.107, f32[256,5]{0,1:T(8,128)S(1)} %fusion.10), channel_id=1, replica_groups=mesh['gx'=2,'gz'=16] {'gx','gz'}, use_global_device_ids=true, to_apply=%region_2.9 | all-reduce | flops 3072 | bytes 24576 | tf_op jit(solution)/shard_map/psum | solution.py:128
  149.1 5.0 %copy.120 = f32[5,2,4,8,4,4,1]{6,5,4,3,2,1,0:T(4,128)} copy(f32[5,2,4,8,4,4,1]{3,5,4,2,1,0,6:T(4,128)S(1)} %fusion.26) | data formatting | bytes 40960 | tf_op jit(solution)/shard_map/stack | solution.py:59
  154.1 5.0 %copy.119 = f32[5,2,4,8,4,4,1]{6,5,4,3,2,1,0:T(4,128)} copy(f32[5,2,4,8,4,4,1]{3,5,4,2,1,0,6:T(4,128)S(1)} %fusion.24) | data formatting | bytes 40960 | tf_op jit(solution)/shard_map/stack | solution.py:59
  159.1 2.8 %fusion.16 = (f32[5,2,4,8,4,1,4]{3,6,4,2,1,0,5:T(4,128)}, f32[5,2,4,8,1,4,4]{3,6,5,2,1,0,4:T(4,128)}, f32[5,2,4,8,1,4,4]{3,6,5,2,1,0,4:T(4,128)}, f32[5,2,4,8,4,1,4]{3,6,4,2,1,0,5:T(4,128)}) fusion(f32[5,2,4,8,4,4,4]{3,6,5,4,2,1,0:T(4,128)S(1)} %bitcast.146, f32[5,2,4,7,4,4]{3,5,4,2,1,0:T(4,128)S(1)} %get-tuple-element.95, ...), kind=kLoop, calls=%fused_computation.30 | loop fusion | flops 61440 | bytes 245760 | tf_op jit(solution)/shard_map/stack | solution.py:59
  161.9 2.1 %copy.114 = f32[5,2,4,8,4,1,4]{6,5,4,3,2,1,0:T(1,128)S(1)} copy(f32[5,2,4,8,4,1,4]{3,6,4,2,1,0,5:T(4,128)} %get-tuple-element.89) | data formatting | bytes 40960 | tf_op jit(solution)/shard_map/stack | solution.py:59
  164.0 2.9 %copy.105 = f32[5,2,4,8,1,4,4]{6,5,4,3,2,1,0:T(4,128)} copy(f32[5,2,4,8,1,4,4]{3,6,5,2,1,0,4:T(4,128)} %get-tuple-element.90) | data formatting | bytes 40960 | tf_op jit(solution)/shard_map/stack | solution.py:59
  166.9 2.8 %copy.104 = f32[5,2,4,8,1,4,4]{6,5,4,3,2,1,0:T(4,128)} copy(f32[5,2,4,8,1,4,4]{3,6,5,2,1,0,4:T(4,128)} %get-tuple-element.91) | data formatting | bytes 40960 | tf_op jit(solution)/shard_map/stack | solution.py:59
  169.7 2.7 %copy.115 = f32[5,2,4,8,4,1,4]{6,5,4,3,2,1,0:T(1,128)} copy(f32[5,2,4,8,4,1,4]{3,6,4,2,1,0,5:T(4,128)} %get-tuple-element.92) | data formatting | bytes 40960 | tf_op jit(solution)/shard_map/stack | solution.py:59
  172.4 6.1 %fusion.7 = f32[5,2,4,8,4,4,4]{6,5,4,3,2,1,0:T(4,128)} fusion(f32[5,2,4,8,1,4,4]{6,5,4,3,2,1,0:T(4,128)} %copy.105, f32[5,2,4,8,1,4,4]{6,5,4,3,2,1,0:T(4,128)} %copy.104, f32[5,2,4,8,4,1,4]{6,5,4,3,2,1,0:T(1,128)} %copy.115, f32[5,2,4,8,4,1,4]{6,5,4,3,2,1,0:T(1,128)S(1)} %copy.114, f32[5,2,4,8,4,4,1]{6,5,4,3,2,1,0:T(4,128)S(1)} %copy-done.1, ...), kind=kLoop, calls=%fused_computation.18 | loop fusion | flops 184320 | bytes 204816 | tf_op jit(solution)/shard_map/mul | solution.py:125
  178.5 4.1 %mul.169 = f32[5,2,4,512]{3,2,1,0:T(4,128)S(1)} reshape(f32[5,2,4,8,4,4,4]{6,5,4,3,2,1,0:T(4,128)} %fusion.7) | data formatting | bytes 163840 | tf_op jit(solution)/shard_map/mul | solution.py:125
  184.2 20.4 %all-reduce.3.cloned.1.call-done = f32[256,256]{1,0:T(8,128)} async-done(((f32[256,256]{1,0:T(8,128)}), f32[256,256]{1,0:T(8,128)}) %all-reduce.3.cloned.1.call-update) | async-done | bytes 262160 | tf_op jit(solution)/shard_map/psum | solution.py:128
  (65 shorter events, 28.7 us)
Async XLA Ops:
  7.2 63.4 %copy-start = (bf16[256,256]{1,0:T(8,128)(2,1)S(1)}, bf16[256,256]{1,0:T(8,128)(2,1)}, u32[]{:S(2)}) copy-start(bf16[256,256]{1,0:T(8,128)(2,1)} %param.27) | copy-start | bytes 393220
  7.2 197.4 %all-reduce.3.cloned.1.call-start = ((), (), s32[]{:S(2)}) async-start(), calls=%async_computation | async-start | bytes 524288 | tf_op jit(solution)/shard_map/psum | solution.py:128
  10.1 14.2 %copy-start.4 = (f32[5,2,4,512]{3,2,1,0:T(4,128)S(1)}, f32[5,2,4,512]{3,2,1,0:T(4,128)}, u32[]{:S(2)}) copy-start(f32[5,2,4,512]{3,2,1,0:T(4,128)} %param.21) | copy-start | bytes 245764
  10.1 54.8 %copy-start.5 = (f32[5,256]{1,0:T(8,128)S(1)}, f32[5,256]{1,0:T(8,128)}, u32[]{:S(2)}) copy-start(f32[5,256]{1,0:T(8,128)} %param.25) | copy-start | bytes 15364
  10.1 54.8 %copy-start.9 = (f32[256]{0:T(256)S(1)}, f32[256]{0:T(256)}, u32[]{:S(2)}) copy-start(f32[256]{0:T(256)} %param.26) | copy-start | bytes 3076
  14.2 132.4 %collective-permute-start.2 = (f32[5,2,1,8,4,4]{3,5,4,2,1,0:T(4,128)}, f32[5,2,1,8,4,4]{3,5,4,2,1,0:T(4,128)}, u32[]{:S(2)}, u32[]{:S(2)}) collective-permute-start(f32[5,2,1,8,4,4]{3,5,4,2,1,0:T(4,128)} %bitcast.21), channel_id=1, source_target_pairs={{0,1},{1,2},{2,3},{3,4},{4,5},{5,6},{6,7},{7,8},{8,9},{9,10},{10,1... | collective-permute-start | bytes 15368 | tf_op jit(solution)/shard_map/ppermute | solution.py:21
  15.5 143.6 %collective-permute-start = (f32[5,1,4,8,4,4]{3,5,4,2,1,0:T(4,128)}, f32[5,1,4,8,4,4]{3,5,4,2,1,0:T(4,128)}, u32[]{:S(2)}, u32[]{:S(2)}) collective-permute-start(f32[5,1,4,8,4,4]{3,5,4,2,1,0:T(4,128)} %get-tuple-element.97), channel_id=1, source_target_pairs={{0,16},{16,0},{1,17},{17,1},{2,18},{18,2},{3,19},{19,3},{4,20},{20... | collective-permute-start | bytes 30728 | tf_op jit(solution)/shard_map/ppermute | solution.py:21
  18.1 141.0 %collective-permute-start.1 = (f32[5,1,4,8,4,4]{3,5,4,2,1,0:T(4,128)}, f32[5,1,4,8,4,4]{3,5,4,2,1,0:T(4,128)}, u32[]{:S(2)}, u32[]{:S(2)}) collective-permute-start(f32[5,1,4,8,4,4]{3,5,4,2,1,0:T(4,128)} %get-tuple-element.98), channel_id=1, source_target_pairs={{16,0},{0,16},{17,1},{1,17},{18,2},{2,18},{19,3},{3,19},{20,4},{4,... | collective-permute-start | bytes 30728 | tf_op jit(solution)/shard_map/ppermute | solution.py:23
  20.1 127.8 %collective-permute-start.3 = (f32[5,2,1,8,4,4]{3,5,4,2,1,0:T(4,128)}, f32[5,2,1,8,4,4]{3,5,4,2,1,0:T(4,128)}, u32[]{:S(2)}, u32[]{:S(2)}) collective-permute-start(f32[5,2,1,8,4,4]{3,5,4,2,1,0:T(4,128)} %slice.191), channel_id=1, source_target_pairs={{1,0},{2,1},{3,2},{4,3},{5,4},{6,5},{7,6},{8,7},{9,8},{10,9},{11,1... | collective-permute-start | bytes 15368 | tf_op jit(solution)/shard_map/ppermute | solution.py:23
  64.9 5.7 %copy-start.6 = (f32[256]{0:T(256)S(1)}, f32[256]{0:T(256)}, u32[]{:S(2)}) copy-start(f32[256]{0:T(256)} %param.28) | copy-start | bytes 3076
  70.6 2.7 %copy-start.8 = (bf16[256,5]{0,1:T(8,128)(2,1)S(1)}, bf16[256,5]{0,1:T(8,128)(2,1)}, u32[]{:S(2)}) copy-start(bf16[256,5]{0,1:T(8,128)(2,1)} %param.29) | copy-start | bytes 7684
  71.3 2.0 copy-start.2
  75.7 1.4 copy-start.10
  80.5 3.6 %copy-start.11 = (bf16[256,4096]{0,1:T(8,128)(2,1)S(1)}, bf16[256,4096]{0,1:T(8,128)(2,1)}, u32[]{:S(2)}) copy-start(bf16[256,4096]{0,1:T(8,128)(2,1)} %copy-done.10) | copy-start | bytes 6291460
  80.5 4.1 %copy-start.12 = (f32[256,4096]{0,1:T(8,128)S(1)}, f32[256,4096]{0,1:T(8,128)}, u32[]{:S(2)}) copy-start(f32[256,4096]{0,1:T(8,128)} %get-tuple-element.104) | copy-start | bytes 12582916
  87.0 5.4 %copy-start.7 = (s32[2,2,4]{2,1,0:T(2,128)S(1)}, s32[2,2,4]{2,1,0:T(2,128)}, u32[]{:S(2)}) copy-start(s32[2,2,4]{2,1,0:T(2,128)} %param.24) | copy-start | bytes 196
  161.9 10.5 %copy-start.1 = (f32[5,2,4,8,4,4,1]{6,5,4,3,2,1,0:T(4,128)S(1)}, f32[5,2,4,8,4,4,1]{6,5,4,3,2,1,0:T(4,128)}, u32[]{:S(2)}) copy-start(f32[5,2,4,8,4,4,1]{6,5,4,3,2,1,0:T(4,128)} %copy.120) | copy-start | bytes 61444
  172.4 10.2 %copy-start.3 = (f32[5,2,4,512]{3,2,1,0:T(4,128)S(1)}, f32[5,2,4,512]{3,2,1,0:T(4,128)}, u32[]{:S(2)}) copy-start(f32[5,2,4,512]{3,2,1,0:T(4,128)} %mul.186) | copy-start | bytes 245764
Sparse Core Ops, SparseCore 0:
  78.6 125.9 all-reduce.2
where the time goes:
time: 214 us; the launch traced here: 213 us
  blocking collectives  80.9 us (38%)
  local copies, waits for them, and re-layouts  45.3 us (21%)
  matrix products  24.4 us (11%)
  waiting for transfers between devices  20.4 us (10%)
  other arithmetic  19.9 us (9%)
  between operations  14.9 us (7%)
  starting transfers between devices  7.2 us (3%)
    psum x1, blocking collectives, per_device(): lax.psum((grad_in, grad_bin, grad_mid, grad_bmid, grad_out), ('gx', 'gz'))  42.5 us
    psum x1, blocking collectives, per_device(): sum_squares = lax.psum(jnp.sum(state * state), ('gx', 'gz'))  38.4 us
    another operation x8, local copies, waits for them, and re-layouts, face_terms(): jnp.stack([lower_term, zero_face, zero_face, upper_term], axis=face_axis)  20.6 us
    psum x1, waiting for transfers between devices, per_device(): lax.psum((grad_in, grad_bin, grad_mid, grad_bmid, grad_out), ('gx', 'gz'))  20.4 us
    dot_general x3, matrix products, inner_rows(): lax.dot_general(first_op, second_op, (((1,), (1,)), ((), ())), precision=...  6.72 us
    dot_general x2, matrix products, inner_first(): lax.dot_general(first_op, second_op, (((0,), (0,)), ((), ())), precision=...  6.37 us
    mul x1, other arithmetic, per_device(): KAPPA * coupled  6.12 us
    another operation x3, other arithmetic, face_terms(): jnp.stack([lower_term, zero_face, zero_face, upper_term], axis=face_axis)  5.25 us
  transfers between devices with their start and end apart: 5, of which 1 were waited for; matrix products, arithmetic and copies ran while one was open for 36% of the time, Pallas kernels for 0%

commit v1 on v0

v1 whole, which is shorter than its diff:
```python
import functools
import math

import jax
import jax.numpy as jnp
from jax import lax
from jax.experimental import pallas as pl
from jax.experimental.pallas import tpu as pltpu
from jax.sharding import PartitionSpec as P

KAPPA = 0.5
DT_STEP = 0.5
EPS = 1e-06
F32 = jnp.float32
BF16 = jnp.bfloat16
MESH = pl.DeviceIdType.MESH


def nt_dot(first_op, second_op):
    return lax.dot_general(
        first_op, second_op, (((1,), (1,)), ((), ())), preferred_element_type=F32
    )


def nn_dot(first_op, second_op):
    return jnp.dot(first_op, second_op, preferred_element_type=F32)


def rounded(value):
    return value.astype(BF16).astype(F32)


def kernel(
    dims,
    state_ref,
    cot_ref,
    inv_ref,
    tags_ref,
    w_in_ref,
    b_in_ref,
    w_mid_ref,
    b_mid_ref,
    w_out_ref,
    gstate_ref,
    gin_ref,
    gbin_ref,
    gmid_ref,
    gbmid_ref,
    gout_ref,
    state_rows,
    grad_rows,
    adj_rows,
    back_rows,
    low_x,
    up_x,
    low_z,
    up_z,
    x_send,
    x_halo,
    z_send,
    z_halo,
    w_first,
    w_back,
    w_mid_t,
    bias_mid,
    joint,
    totals,
    totals_in,
    totals_out,
    norm_mine,
    norm_all,
    core_send,
    core_recv,
    plane_send,
    plane_all,
    line_send,
    line_all,
    gathered,
    norm_sems,
    halo_send_sems,
    halo_recv_sems,
    core_sems,
    plane_send_sems,
    plane_recv_sems,
    line_send_sems,
    line_recv_sems,
    spread_send_sems,
    spread_recv_sems,
    pair_send_sems,
    pair_recv_sems,
):
    gx, gz = dims
    channels, x_elems, z_elems, line = state_ref.shape
    hidden = w_mid_ref.shape[0]
    columns = x_elems * z_elems
    count = gx * gz
    half = hidden // 2
    n_plane, n_line = gx * 2, gz // 4
    part = hidden // n_plane
    my_x, my_z = lax.axis_index("gx"), lax.axis_index("gz")
    me = my_x * gz + my_z
    core, side, level = my_z % 2, (my_z // 2) % 2, my_z // 4
    my_plane = my_x * 2 + side
    other_core = (my_x, my_z + 1 - 2 * core)

    barrier = pltpu.get_barrier_semaphore()

    def greet(step, carry):
        to = lax.rem(me + step, count)
        pl.semaphore_signal(
            barrier, inc=1, device_id=(to // gz, lax.rem(to, gz)), device_id_type=MESH
        )
        return carry

    lax.fori_loop(1, count, greet, 0)

    squares = state_ref[...] * state_ref[...]
    squares = jnp.sum(jnp.sum(squares, axis=0), axis=0)
    folded = squares[:, :128]
    for start in range(128, line, 128):
        folded = folded + squares[:, start : start + 128]
    norm_mine[...] = jnp.sum(folded, axis=0, keepdims=True)

    pl.semaphore_wait(barrier, count - 1)

    def norm_copy(step):
        to = lax.rem(me + step, count)
        return pltpu.make_async_remote_copy(
            src_ref=norm_mine,
            dst_ref=norm_all.at[step - 1],
            send_sem=norm_sems.at[0],
            recv_sem=norm_sems.at[1],
            device_id=(to // gz, lax.rem(to, gz)),
            device_id_type=MESH,
        )

    def send_norm(step, carry):
        norm_copy(step).start()
        return carry

    lax.fori_loop(1, count, send_norm, 0)

    for c in range(channels):
        for i in range(x_elems):
            low_x[c, i * z_elems : (i + 1) * z_elems, :] = cot_ref[c, i]
    lane = lax.broadcasted_iota(jnp.int32, (columns, 128), 1)
    first_lane = lane & 64
    blocks = line // 128

    def adjoint_step(n, sums):
        spot = first_lane + n
        rows = jnp.concatenate([inv_ref[n, i] for i in range(x_elems)], axis=0)
        out = []
        for c in range(channels):
            for t in range(blocks):
                piece = low_x[c, :, t * 128 : (t + 1) * 128]
                spread = jnp.take_along_axis(piece, spot, axis=1)
                out.append(
                    sums[c * blocks + t] + rows[:, t * 128 : (t + 1) * 128] * spread
                )
        return tuple(out)

    zero_tile = jnp.zeros((columns, 128), F32)
    sums = lax.fori_loop(
        0, inv_ref.shape[0], adjoint_step, (zero_tile,) * (channels * blocks), unroll=4
    )
    for c in range(channels):
        for t in range(blocks):
            adj_rows[c, :, t * 128 : (t + 1) * 128] = sums[c * blocks + t]

    for c in range(channels):
        x_send[0, c] = adj_rows[c, 0:z_elems, :]
        x_send[1, c] = adj_rows[c, columns - z_elems : columns, :]
        for i in range(x_elems):
            z_send[0, c * x_elems + i] = adj_rows[c, i * z_elems : i * z_elems + 1, :]
            z_send[1, c * x_elems + i] = adj_rows[
                c, (i + 1) * z_elems - 1 : (i + 1) * z_elems, :
            ]
    halo_copies = []
    for spot, (src, dst, to) in enumerate(
        (
            (x_send.at[0], x_halo.at[1], (lax.rem(my_x + gx - 1, gx), my_z)),
            (x_send.at[1], x_halo.at[0], (lax.rem(my_x + 1, gx), my_z)),
            (z_send.at[0], z_halo.at[1], (my_x, lax.rem(my_z + gz - 1, gz))),
            (z_send.at[1], z_halo.at[0], (my_x, lax.rem(my_z + 1, gz))),
        )
    ):
        copy = pltpu.make_async_remote_copy(
            src_ref=src,
            dst_ref=dst,
            send_sem=halo_send_sems.at[spot],
            recv_sem=halo_recv_sems.at[spot],
            device_id=to,
            device_id_type=MESH,
        )
        copy.start()
        halo_copies.append(copy)

    for i in range(x_elems):
        for k in range(z_elems):
            row = i * z_elems + k
            state_rows[row] = jnp.ones((8, line), F32)
            grad_rows[row] = jnp.zeros((16, line), F32)
            for c in range(channels):
                state_rows[row, c : c + 1, :] = state_ref[c, i, k : k + 1, :]
                grad_rows[row, c : c + 1, :] = DT_STEP * adj_rows[c, row : row + 1, :]
    w_in = w_in_ref[...]
    w_high = rounded(w_in)
    w_low = rounded(w_in - w_high)
    b_in = b_in_ref[...]
    b_high = rounded(b_in)
    b_next = rounded(b_in - b_high)
    b_last = rounded(b_in - b_high - b_next)
    joint_rows = jnp.concatenate(
        [w_high, b_high, b_next, b_last, w_high, jnp.zeros((8 - channels, hidden), F32)]
        + [w_low, jnp.zeros((16 - channels, hidden), F32)],
        axis=0,
    )
    w_first[...] = joint_rows.T.astype(BF16)
    w_back[...] = jnp.concatenate([joint_rows[8:16], joint_rows[16:24]], axis=0).astype(BF16)
    w_mid_t[...] = w_mid_ref[...].astype(F32).T.astype(BF16)
    bias_mid[...] = jnp.broadcast_to(b_mid_ref[...], (line, hidden)).T[:, :]
    totals[...] = jnp.zeros_like(totals)
    totals_in[...] = jnp.zeros_like(totals_in)
    totals_out[...] = jnp.zeros_like(totals_out)

    whole = norm_all.at[pl.ds(0, count - 1)]
    pltpu.make_async_copy(whole, whole, norm_sems.at[0]).wait()
    pltpu.make_async_copy(whole, whole, norm_sems.at[1]).wait()
    sum_squares = norm_mine[...] + jnp.sum(norm_all[0 : count - 1], axis=0)
    sum_squares = jnp.sum(sum_squares, axis=1, keepdims=True)
    entry_count = channels * columns * line * count
    inv_norm = lax.rsqrt(sum_squares / entry_count + EPS)
    row_index = lax.broadcasted_iota(jnp.int32, (8, line), 0)
    scale = jnp.where(row_index < channels, jnp.broadcast_to(inv_norm, (8, line)), 1.0)

    def column(row, carry):
        scaled = state_rows[row] * scale
        high = rounded(scaled)
        low = scaled - high
        inputs = jnp.concatenate([high, low, high, jnp.zeros_like(high)], axis=0).astype(BF16)
        joint[hidden:, :] = inputs
        pre = nn_dot(w_first[...], inputs)
        gate = 0.5 * jnp.tanh(0.5 * pre) + 0.5
        act = pre * gate
        slope_one = gate + act * (1.0 - gate)
        hidden_one = act.astype(BF16)
        joint[:hidden, :] = hidden_one
        pre = nn_dot(w_mid_t[...], hidden_one) + bias_mid[...]
        gate = 0.5 * jnp.tanh(0.5 * pre) + 0.5
        act = pre * gate
        slope_two = gate + act * (1.0 - gate)
        hidden_two = act.astype(BF16)
        out_grad = grad_rows[row].astype(BF16)
        totals_out[...] += nt_dot(out_grad, hidden_two)
        back_two = nn_dot(w_out_ref[...], out_grad[:channels])
        delta_two = (back_two * slope_two).astype(BF16)
        totals[...] += nt_dot(joint[...], delta_two)
        delta_one = (nn_dot(w_mid_ref[...], delta_two) * slope_one).astype(BF16)
        totals_in[...] += nt_dot(inputs, delta_one)
        back = nn_dot(w_back[...], delta_one)
        back = back[:8] + back[8:]
        for c in range(channels):
            back_rows[c, pl.ds(row, 1), :] = back[c : c + 1, :]
        return carry

    lax.fori_loop(0, columns, column, 0)

    top = lax.broadcasted_iota(jnp.int32, (8, hidden), 0)
    mixed = jnp.where(
        top == channels + 1, totals[hidden : hidden + 8], totals_in[0:8] + totals_in[8:16]
    )
    for h in range(2):
        lanes = slice(h * half, (h + 1) * half)
        core_send[h, 0:hidden, :] = totals[0:hidden, lanes]
        core_send[h, hidden : hidden + 8, :] = mixed[:, lanes]
        core_send[h, hidden + 8 : hidden + 16, :] = totals_out[0:8, lanes]
    core_copy = pltpu.make_async_remote_copy(
        src_ref=core_send.at[1 - core],
        dst_ref=core_recv,
        send_sem=core_sems.at[0],
        recv_sem=core_sems.at[1],
        device_id=other_core,
        device_id_type=MESH,
    )
    core_copy.start()

    for copy in halo_copies:
        copy.wait()
    for c in range(channels):
        low_x[c, 0:z_elems, :] = x_halo[0, c]
        up_x[c, columns - z_elems : columns, :] = x_halo[1, c]
        if x_elems > 1:
            low_x[c, z_elems:columns, :] = adj_rows[c, 0 : columns - z_elems, :]
            up_x[c, 0 : columns - z_elems, :] = adj_rows[c, z_elems:columns, :]
        for i in range(x_elems):
            first, last = i * z_elems, (i + 1) * z_elems
            low_z[c, first : first + 1, :] = z_halo[0, c * x_elems + i]
            up_z[c, last - 1 : last, :] = z_halo[1, c * x_elems + i]
            if z_elems > 1:
                low_z[c, first + 1 : last, :] = adj_rows[c, first : last - 1, :]
                up_z[c, first : last - 1, :] = adj_rows[c, first + 1 : last, :]
    lane = lax.broadcasted_iota(jnp.int32, (columns, line), 1)
    row = lax.broadcasted_iota(jnp.int32, (columns, line), 0)
    spot_a, spot_b, spot_c, spot_j = (lane >> 4) & 3, (lane >> 2) & 3, lane & 3, lane >> 6
    bottom = jnp.zeros((columns, line), F32)
    ceiling = jnp.zeros((columns, line), F32)
    for i in range(x_elems):
        for k in range(z_elems):
            here = row == i * z_elems + k
            bottom = jnp.where(here, -2.0 * tags_ref[0, i, k].astype(F32), bottom)
            ceiling = jnp.where(here, -2.0 * tags_ref[1, i, k].astype(F32), ceiling)
    for c in range(channels):
        own = adj_rows[c]
        low_y = jnp.where(spot_j == 0, bottom * own, pltpu.roll(own, 52, 1) - own)
        up_y = jnp.where(
            spot_j == line // 64 - 1, ceiling * own, pltpu.roll(own, line - 52, 1) - own
        )
        jump = (
            jnp.where(spot_a == 0, pltpu.roll(low_x[c], line - 48, 1) - own, 0.0)
            + jnp.where(spot_a == 3, pltpu.roll(up_x[c], 48, 1) - own, 0.0)
            + jnp.where(spot_b == 0, low_y, 0.0)
            + jnp.where(spot_b == 3, up_y, 0.0)
            + jnp.where(spot_c == 0, pltpu.roll(low_z[c], line - 3, 1) - own, 0.0)
            + jnp.where(spot_c == 3, pltpu.roll(up_z[c], 3, 1) - own, 0.0)
        )
        back_rows[c] = own + 0.5 * KAPPA * jump + inv_norm * back_rows[c]
        for i in range(x_elems):
            gstate_ref[c, i] = back_rows[c, i * z_elems : (i + 1) * z_elems, :]

    core_copy.wait()
    for q in range(n_plane):
        mine = core_send[core, q * part : (q + 1) * part, :]
        plane_send[q, 0:part, :] = mine + core_recv[q * part : (q + 1) * part, :]
        plane_send[q, part:, :] = core_send[core, hidden:, :] + core_recv[hidden:, :]
    plane_copies = []
    for d in range(1, n_plane):
        to = lax.rem(my_plane + d, n_plane)
        copy = pltpu.make_async_remote_copy(
            src_ref=plane_send.at[to],
            dst_ref=plane_all.at[my_plane],
            send_sem=plane_send_sems.at[d],
            recv_sem=plane_recv_sems.at[d],
            device_id=(to // 2, level * 4 + lax.rem(to, 2) * 2 + core),
            device_id_type=MESH,
        )
        copy.start()
        plane_copies.append(copy)
    plane_all[my_plane] = plane_send[my_plane]
    for copy in plane_copies:
        copy.wait()
    line_send[...] = sum((plane_all[q] for q in range(1, n_plane)), plane_all[0])
    line_copies = []
    for d in range(1, n_line):
        to = lax.rem(level + d, n_line)
        copy = pltpu.make_async_remote_copy(
            src_ref=line_send,
            dst_ref=line_all.at[level],
            send_sem=line_send_sems.at[d],
            recv_sem=line_recv_sems.at[d],
            device_id=(my_x, to * 4 + side * 2 + core),
            device_id_type=MESH,
        )
        copy.start()
        line_copies.append(copy)
    line_all[level] = line_send[...]
    for copy in line_copies:
        copy.wait()
    factor = 4.0 / math.sqrt(entry_count // channels)
    result = sum((line_all[r] for r in range(1, n_line)), line_all[0])
    gathered[core, my_plane] = factor * result

    def to_pair(slot, d):
        return pltpu.make_async_remote_copy(
            src_ref=gathered.at[core, slot],
            dst_ref=gathered.at[core, slot],
            send_sem=pair_send_sems.at[d],
            recv_sem=pair_recv_sems.at[d],
            device_id=other_core,
            device_id_type=MESH,
        )

    spread_copies = []
    for d in range(1, n_plane):
        to = lax.rem(my_plane + d, n_plane)
        copy = pltpu.make_async_remote_copy(
            src_ref=gathered.at[core, my_plane],
            dst_ref=gathered.at[core, my_plane],
            send_sem=spread_send_sems.at[d],
            recv_sem=spread_recv_sems.at[d],
            device_id=(to // 2, level * 4 + lax.rem(to, 2) * 2 + core),
            device_id_type=MESH,
        )
        copy.start()
        spread_copies.append(copy)
    pair_copies = [to_pair(my_plane, 0)]
    pair_copies[0].start()
    for d in range(1, n_plane):
        spread_copies[d - 1].wait_recv()
        copy = to_pair(lax.rem(my_plane + n_plane - d, n_plane), d)
        copy.start()
        pair_copies.append(copy)
    for copy in spread_copies:
        copy.wait_send()
    for copy in pair_copies:
        copy.wait()
    for h in range(2):
        lanes = slice(h * half, (h + 1) * half)
        for q in range(n_plane):
            gmid_ref[q * part : (q + 1) * part, lanes] = gathered[h, q, 0:part, :]
        small = gathered[h, 0, part : part + 8, :]
        gin_ref[:, lanes] = small[0:channels]
        gbin_ref[:, lanes] = small[channels : channels + 1]
        gbmid_ref[:, lanes] = small[channels + 1 : channels + 2]
        gout_ref[lanes, :] = gathered[h, 0, part + 8 : part + 16, :].T[:, 0:channels]


def per_device(dims, state, cotangent, local_inverse, wall_tags, w_in, b_in, w_mid, b_mid, w_out):
    gx, gz = dims
    channels, x_elems, z_elems, line = state.shape
    hidden = w_mid.shape[0]
    columns = x_elems * z_elems
    n_plane, n_line = gx * 2, gz // 4
    part = hidden // n_plane
    half = hidden // 2
    vmem = pl.BlockSpec(memory_space=pltpu.VMEM)
    smem = pl.BlockSpec(memory_space=pltpu.SMEM)
    rows = pltpu.VMEM((channels, columns, line), F32)
    dma = pltpu.SemaphoreType.DMA
    out = pl.pallas_call(
        functools.partial(kernel, dims),
        out_shape=(
            jax.ShapeDtypeStruct(state.shape, F32),
            jax.ShapeDtypeStruct((channels, hidden), F32),
            jax.ShapeDtypeStruct((1, hidden), F32),
            jax.ShapeDtypeStruct((hidden, hidden), F32),
            jax.ShapeDtypeStruct((1, hidden), F32),
            jax.ShapeDtypeStruct((hidden, channels), F32),
        ),
        in_specs=[vmem, vmem, vmem, smem] + [vmem] * 5,
        out_specs=(vmem,) * 6,
        scratch_shapes=[
            pltpu.VMEM((columns, 8, line), F32),
            pltpu.VMEM((columns, 16, line), F32),
            rows,
            rows,
            rows,
            rows,
            rows,
            rows,
            pltpu.VMEM((2, channels, z_elems, line), F32),
            pltpu.VMEM((2, channels, z_elems, line), F32),
            pltpu.VMEM((2, channels * x_elems, 1, line), F32),
            pltpu.VMEM((2, channels * x_elems, 1, line), F32),
            pltpu.VMEM((hidden, 32), BF16),
            pltpu.VMEM((16, hidden), BF16),
            pltpu.VMEM((hidden, hidden), BF16),
            pltpu.VMEM((hidden, line), F32),
            pltpu.VMEM((hidden + 32, line), BF16),
            pltpu.VMEM((hidden + 32, hidden), F32),
            pltpu.VMEM((32, hidden), F32),
            pltpu.VMEM((16, hidden), F32),
            pltpu.VMEM((1, 128), F32),
            pltpu.VMEM((gx * gz, 1, 128), F32),
            pltpu.VMEM((2, hidden + 16, half), F32),
            pltpu.VMEM((hidden + 16, half), F32),
            pltpu.VMEM((n_plane, part + 16, half), F32),
            pltpu.VMEM((n_plane, part + 16, half), F32),
            pltpu.VMEM((part + 16, half), F32),
            pltpu.VMEM((n_line, part + 16, half), F32),
            pltpu.VMEM((2, n_plane, part + 16, half), F32),
            dma((2,)),
            dma((4,)),
            dma((4,)),
            dma((2,)),
            dma((n_plane,)),
            dma((n_plane,)),
            dma((n_line,)),
            dma((n_line,)),
            dma((n_plane,)),
            dma((n_plane,)),
            dma((n_plane,)),
            dma((n_plane,)),
        ],
        compiler_params=pltpu.CompilerParams(
            collective_id=0, has_side_effects=True, vmem_limit_bytes=40 * 1024 * 1024
        ),
    )(
        state,
        cotangent,
        local_inverse,
        wall_tags,
        w_in,
        b_in.reshape(1, hidden),
        w_mid,
        b_mid.reshape(1, hidden),
        w_out,
    )
    return out[0], out[1], out[2].reshape(hidden), out[3], out[4].reshape(hidden), out[5]


def solution(mesh):
    placed = (
        P(None, "gx", "gz", None),
        P(None, "gx", "gz", None),
        P(None, "gx", "gz", None),
        P(None, "gx", "gz"),
        P(),
        P(),
        P(),
        P(),
        P(),
    )
    return jax.shard_map(
        functools.partial(per_device, (mesh.shape["gx"], mesh.shape["gz"])),
        mesh=mesh,
        in_specs=placed,
        out_specs=(P(None, "gx", "gz", None), P(), P(), P(), P(), P()),
        check_vma=False,
    )
```

time: 214 us -> 45.2 us (0.21)
  blocking collectives: 80.9 us -> 0 us
  local copies, waits for them, and re-layouts: 45.3 us -> 8.5 us
  Pallas kernels: 0 us -> 35.7 us
  matrix products: 24.4 us -> 0 us
  waiting for transfers between devices: 20.4 us -> 0 us
  other arithmetic: 19.9 us -> 0 us
  between operations: 14.9 us -> 0.71 us
  starting transfers between devices: 7.2 us -> 0 us
    psum x2 -> x0, blocking collectives: 80.9 us -> none  [the longest x1 42.5 us: per_device(): lax.psum((grad_in, grad_bin, grad_mid, grad_bmid, grad_out), ('gx', 'gz'))]
    pallas_call x0 -> x1, Pallas kernels: none -> 35.7 us  [per_device(): pl.pallas_call(functools.partial(kernel, dims), out_shape=(jax.ShapeDtype...]
    dot_general x9 -> x0, matrix products: 24.4 us -> none  [the longest x3 6.72 us: inner_rows(): lax.dot_general(first_op, second_op, (((1,), (1,)), ((), ())), precision=...]
    another operation x9 -> x0, local copies, waits for them, and re-layouts: 22.1 us -> none  [the longest x8 20.6 us: face_terms(): jnp.stack([lower_term, zero_face, zero_face, upper_term], axis=face_axis)]
    psum x1 -> x0, waiting for transfers between devices: 20.4 us -> none  [per_device(): lax.psum((grad_in, grad_bin, grad_mid, grad_bmid, grad_out), ('gx', 'gz'))]
    mul x7 -> x0, other arithmetic: 11.1 us -> none  [the longest x1 6.12 us: per_device(): KAPPA * coupled]
    ppermute x4 -> x0, starting transfers between devices: 7.16 us -> none  [the longest x2 4.19 us: extended(): lax.ppermute(head, axis, [((i + 1) % count, i) for i in range(count)])]
    slice x6 -> x0, local copies, waits for them, and re-layouts: 5.32 us -> none  [the longest x2 1.72 us: coupling(): blocks_view[:, :, :, :1, :, 0, :]]
  transfers between devices with their start and end apart: 5 -> 0, of which waited for: 1 -> 0; matrix products, arithmetic and copies ran while one was open for 36% -> 0% of each run, Pallas kernels for 0% -> 0%
where the time goes in v1:
time: 45.2 us; the launch traced here: 44.9 us
  Pallas kernels  35.7 us (79%)
  local copies, waits for them, and re-layouts  8.5 us (19%)
  between operations  0.71 us (2%)
    pallas_call x1, Pallas kernels, per_device(): pl.pallas_call(functools.partial(kernel, dims), out_shape=(jax.ShapeDtype...  35.7 us
    unnamed x23, local copies, waits for them, and re-layouts  8.5 us

profile of v1, /device:TPU:0, one launch (start us, length us, event | category | flops | bytes accessed | tf_op | source)
XLA Modules:
  0.0 44.9 jit_solution(4448732657437817512)
XLA Ops:
  0.6 0.0 copy-start.4
  0.6 0.0 copy-start.5
  0.7 0.0 copy-start.6
  0.7 0.0 copy-start.7
  0.7 0.8 %copy.15.w_out_ref = bf16[256,5]{1,0:T(8,128)(2,1)S(1)} copy(bf16[256,5]{0,1:T(8,128)(2,1)} %param.17) | data formatting | bytes 5120 | tf_op args[8]
  1.5 0.0 copy-done.4
  1.5 0.0 copy-done.5
  1.5 0.0 copy-done.6
  1.5 0.0 copy-done.7
  1.6 0.0 copy-start
  1.6 1.2 %copy-done = f32[64,2,4,512]{3,2,1,0:T(4,128)S(1)} copy-done((f32[64,2,4,512]{3,2,1,0:T(4,128)S(1)}, f32[64,2,4,512]{3,2,1,0:T(4,128)}, u32[]{:S(2)}) %copy-start) | copy-done | bytes 1048600
  2.8 0.0 copy-start.1
  2.8 0.9 %copy-done.1 = bf16[256,256]{1,0:T(8,128)(2,1)S(1)} copy-done((bf16[256,256]{1,0:T(8,128)(2,1)S(1)}, bf16[256,256]{1,0:T(8,128)(2,1)}, u32[]{:S(2)}) %copy-start.1) | copy-done | bytes 131096
  3.7 0.0 copy-start.2
  3.7 0.9 %copy-done.2 = f32[5,2,4,512]{3,2,1,0:T(4,128)S(1)} copy-done((f32[5,2,4,512]{3,2,1,0:T(4,128)S(1)}, f32[5,2,4,512]{3,2,1,0:T(4,128)}, u32[]{:S(2)}) %copy-start.2) | copy-done | bytes 81944
  4.6 0.0 copy-start.3
  4.6 0.9 %copy-done.3 = f32[5,2,4,512]{3,2,1,0:T(4,128)S(1)} copy-done((f32[5,2,4,512]{3,2,1,0:T(4,128)S(1)}, f32[5,2,4,512]{3,2,1,0:T(4,128)}, u32[]{:S(2)}) %copy-start.3) | copy-done | bytes 81944
  5.5 35.7 %shard_map.136 = (f32[5,2,4,512]{3,2,1,0:T(4,128)S(1)}, f32[5,256]{1,0:T(8,128)S(1)}, f32[1,256]{1,0:T(1,128)S(1)}, f32[256,256]{1,0:T(8,128)S(1)}, f32[1,256]{1,0:T(1,128)S(1)}, /*index=5*/f32[256,5]{1,0:T(8,128)S(1)}) custom-call(f32[5,2,4,512]{3,2,1,0:T(4,128)S(1)} %copy-done.2, f32[5,2,4,512]{3,2,1,0:T(4,128)S(1)} %copy-done.3, ...), custom_call_target="tpu_custom_call" | custom-call | tf_op jit(solution)/shard_map/pallas_call | solution.py:430
  41.2 0.7 %copy.16 = f32[256,5]{0,1:T(8,128)} copy(f32[256,5]{1,0:T(8,128)S(1)} %get-tuple-element.23) | data formatting | bytes 10240
  41.8 0.6 %copy.22 = f32[5,2,4,512]{3,2,1,0:T(4,128)} copy(f32[5,2,4,512]{3,2,1,0:T(4,128)S(1)} %get-tuple-element.30) | data formatting | bytes 163840
  42.5 0.6 %copy.23 = f32[5,256]{1,0:T(8,128)} copy(f32[5,256]{1,0:T(8,128)S(1)} %get-tuple-element.31) | data formatting | bytes 10240
  43.1 0.6 %copy.24 = f32[256]{0:T(256)} copy(f32[256]{0:T(256)S(1)} %bitcast.5) | data formatting | bytes 2048
  43.6 0.7 %copy.25 = f32[256,256]{1,0:T(8,128)} copy(f32[256,256]{1,0:T(8,128)S(1)} %get-tuple-element.33) | data formatting | bytes 524288
  44.3 0.6 %copy.26 = f32[256]{0:T(256)} copy(f32[256]{0:T(256)S(1)} %bitcast.4) | data formatting | bytes 2048
Async XLA Ops:
  0.6 0.9 %copy-start.4 = (f32[5,256]{1,0:T(8,128)S(1)}, f32[5,256]{1,0:T(8,128)}, u32[]{:S(2)}) copy-start(f32[5,256]{1,0:T(8,128)} %w_in_ref.1) | copy-start | bytes 15364
  0.6 0.9 %copy-start.5 = (s32[2,2,4]{2,1,0:T(2,128)S(1)}, s32[2,2,4]{2,1,0:T(2,128)}, u32[]{:S(2)}) copy-start(s32[2,2,4]{2,1,0:T(2,128)} %tags_ref.1) | copy-start | bytes 196
  0.7 0.9 %copy-start.6 = (f32[256]{0:T(256)S(1)}, f32[256]{0:T(256)}, u32[]{:S(2)}) copy-start(f32[256]{0:T(256)} %param.14) | copy-start | bytes 3076
  0.7 0.9 %copy-start.7 = (f32[256]{0:T(256)S(1)}, f32[256]{0:T(256)}, u32[]{:S(2)}) copy-start(f32[256]{0:T(256)} %param.16) | copy-start | bytes 3076
  1.6 1.2 %copy-start = (f32[64,2,4,512]{3,2,1,0:T(4,128)S(1)}, f32[64,2,4,512]{3,2,1,0:T(4,128)}, u32[]{:S(2)}) copy-start(f32[64,2,4,512]{3,2,1,0:T(4,128)} %inv_ref.1) | copy-start | bytes 3145732
  2.8 0.9 %copy-start.1 = (bf16[256,256]{1,0:T(8,128)(2,1)S(1)}, bf16[256,256]{1,0:T(8,128)(2,1)}, u32[]{:S(2)}) copy-start(bf16[256,256]{1,0:T(8,128)(2,1)} %w_mid_ref.1) | copy-start | bytes 393220
  3.7 0.9 %copy-start.2 = (f32[5,2,4,512]{3,2,1,0:T(4,128)S(1)}, f32[5,2,4,512]{3,2,1,0:T(4,128)}, u32[]{:S(2)}) copy-start(f32[5,2,4,512]{3,2,1,0:T(4,128)} %state_ref.1) | copy-start | bytes 245764
  4.6 0.9 %copy-start.3 = (f32[5,2,4,512]{3,2,1,0:T(4,128)S(1)}, f32[5,2,4,512]{3,2,1,0:T(4,128)}, u32[]{:S(2)}) copy-start(f32[5,2,4,512]{3,2,1,0:T(4,128)} %cot_ref.1) | copy-start | bytes 245764

commit v2 on v1

v2 whole, which is shorter than its diff:
```python
import functools
import math

import jax
import jax.numpy as jnp
from jax import lax
from jax.experimental import pallas as pl
from jax.experimental.pallas import tpu as pltpu
from jax.sharding import PartitionSpec as P

KAPPA = 0.5
DT_STEP = 0.5
EPS = 1e-06
F32 = jnp.float32
BF16 = jnp.bfloat16
MESH = pl.DeviceIdType.MESH


def nt_dot(first_op, second_op):
    return lax.dot_general(
        first_op, second_op, (((1,), (1,)), ((), ())), preferred_element_type=F32
    )


def nn_dot(first_op, second_op):
    return jnp.dot(first_op, second_op, preferred_element_type=F32)


def rounded(value):
    return value.astype(BF16).astype(F32)


def kernel(
    dims,
    state_hbm,
    cot_hbm,
    inv_hbm,
    tags_hbm,
    w_in_hbm,
    b_in_hbm,
    w_mid_hbm,
    b_mid_hbm,
    w_out_ref,
    gstate_hbm,
    gin_hbm,
    gbin_hbm,
    gmid_hbm,
    gbmid_hbm,
    gout_hbm,
    gstate_ref,
    gin_ref,
    gbin_ref,
    gbmid_ref,
    gout_ref,
    gathered,
    gathered_ext,
    state_ref,
    cot_ref,
    inv_ref,
    tags_ref,
    w_in_ref,
    b_in_ref,
    w_mid_ref,
    b_mid_ref,
    state_rows,
    grad_rows,
    adj_rows,
    back_rows,
    low_x,
    up_x,
    low_z,
    up_z,
    x_send,
    x_halo,
    z_send,
    z_halo,
    w_first,
    w_back,
    w_mid_t,
    w_mid_half,
    w_out_half,
    bias_mid,
    joint_even,
    joint_odd,
    slope_even,
    slope_odd,
    delta_even,
    delta_odd,
    totals,
    totals_in,
    totals_out,
    norm_mine,
    norm_all,
    core_send,
    core_recv,
    plane_send,
    plane_all,
    line_send,
    line_all,
    ext_core_send,
    ext_core_recv,
    ext_plane_send,
    ext_plane_all,
    ext_line_send,
    ext_line_all,
    load_sems,
    store_sems,
    norm_sems,
    halo_send_sems,
    halo_recv_sems,
    core_sems,
    plane_send_sems,
    plane_recv_sems,
    line_send_sems,
    line_recv_sems,
    ext_core_sems,
    ext_plane_send_sems,
    ext_plane_recv_sems,
    ext_line_send_sems,
    ext_line_recv_sems,
    spread_send_sems,
    spread_recv_sems,
    pair_send_sems,
    pair_recv_sems,
):
    gx, gz = dims
    channels, x_elems, z_elems, line = state_ref.shape
    hidden = w_mid_ref.shape[0]
    columns = x_elems * z_elems
    count = gx * gz
    half = hidden // 2
    n_plane, n_line = gx * 2, gz // 4
    part = hidden // n_plane
    nodes = inv_ref.shape[0]
    pieces = 4
    piece = nodes // pieces
    my_x, my_z = lax.axis_index("gx"), lax.axis_index("gz")
    me = my_x * gz + my_z
    core, side, level = my_z % 2, (my_z // 2) % 2, my_z // 4
    my_plane = my_x * 2 + side
    other_core = (my_x, my_z + 1 - 2 * core)

    loads = [
        pltpu.make_async_copy(src, dst, load_sems.at[spot])
        for spot, (src, dst) in enumerate(
            (
                (state_hbm, state_ref),
                (cot_hbm, cot_ref),
                (w_in_hbm, w_in_ref),
                (b_in_hbm, b_in_ref),
                (w_mid_hbm, w_mid_ref),
                (b_mid_hbm, b_mid_ref),
                (tags_hbm, tags_ref),
            )
        )
    ]
    inv_loads = [
        pltpu.make_async_copy(
            inv_hbm.at[pl.ds(p * piece, piece)],
            inv_ref.at[pl.ds(p * piece, piece)],
            load_sems.at[len(loads) + p],
        )
        for p in range(pieces)
    ]
    for load in loads[:2] + inv_loads + loads[2:]:
        load.start()

    barrier = pltpu.get_barrier_semaphore()

    def greet(step, carry):
        to = lax.rem(me + step, count)
        pl.semaphore_signal(
            barrier, inc=1, device_id=(to // gz, lax.rem(to, gz)), device_id_type=MESH
        )
        return carry

    lax.fori_loop(1, count, greet, 0)

    loads[0].wait()
    squares = state_ref[...] * state_ref[...]
    squares = jnp.sum(jnp.sum(squares, axis=0), axis=0)
    folded = squares[:, :128]
    for start in range(128, line, 128):
        folded = folded + squares[:, start : start + 128]
    norm_mine[...] = jnp.sum(folded, axis=0, keepdims=True)

    pl.semaphore_wait(barrier, count - 1)

    def send_norm(step, carry):
        to = lax.rem(me + step, count)
        pltpu.make_async_remote_copy(
            src_ref=norm_mine,
            dst_ref=norm_all.at[step - 1],
            send_sem=norm_sems.at[0],
            recv_sem=norm_sems.at[1],
            device_id=(to // gz, lax.rem(to, gz)),
            device_id_type=MESH,
        ).start()
        return carry

    lax.fori_loop(1, count, send_norm, 0)

    loads[1].wait()
    for c in range(channels):
        for i in range(x_elems):
            low_x[c, i * z_elems : (i + 1) * z_elems, :] = cot_ref[c, i]
    lane = lax.broadcasted_iota(jnp.int32, (columns, 128), 1)
    first_lane = lane & 64
    blocks = line // 128

    def adjoint_step(n, sums):
        spot = first_lane + n
        rows = jnp.concatenate([inv_ref[n, i] for i in range(x_elems)], axis=0)
        out = []
        for c in range(channels):
            for t in range(blocks):
                tile = low_x[c, :, t * 128 : (t + 1) * 128]
                spread = jnp.take_along_axis(tile, spot, axis=1)
                out.append(
                    sums[c * blocks + t] + rows[:, t * 128 : (t + 1) * 128] * spread
                )
        return tuple(out)

    sums = (jnp.zeros((columns, 128), F32),) * (channels * blocks)
    for p in range(pieces):
        inv_loads[p].wait()
        sums = lax.fori_loop(p * piece, (p + 1) * piece, adjoint_step, sums, unroll=4)
    for c in range(channels):
        for t in range(blocks):
            adj_rows[c, :, t * 128 : (t + 1) * 128] = sums[c * blocks + t]

    for c in range(channels):
        x_send[0, c] = adj_rows[c, 0:z_elems, :]
        x_send[1, c] = adj_rows[c, columns - z_elems : columns, :]
        for i in range(x_elems):
            z_send[0, c * x_elems + i] = adj_rows[c, i * z_elems : i * z_elems + 1, :]
            z_send[1, c * x_elems + i] = adj_rows[
                c, (i + 1) * z_elems - 1 : (i + 1) * z_elems, :
            ]
    halo_copies = []
    for spot, (src, dst, to) in enumerate(
        (
            (x_send.at[0], x_halo.at[1], (lax.rem(my_x + gx - 1, gx), my_z)),
            (x_send.at[1], x_halo.at[0], (lax.rem(my_x + 1, gx), my_z)),
            (z_send.at[0], z_halo.at[1], (my_x, lax.rem(my_z + gz - 1, gz))),
            (z_send.at[1], z_halo.at[0], (my_x, lax.rem(my_z + 1, gz))),
        )
    ):
        copy = pltpu.make_async_remote_copy(
            src_ref=src,
            dst_ref=dst,
            send_sem=halo_send_sems.at[spot],
            recv_sem=halo_recv_sems.at[spot],
            device_id=to,
            device_id_type=MESH,
        )
        copy.start()
        halo_copies.append(copy)

    for load in loads[2:]:
        load.wait()
    for i in range(x_elems):
        for k in range(z_elems):
            row = i * z_elems + k
            state_rows[row] = jnp.ones((8, line), F32)
            grad_rows[row] = jnp.zeros((16, line), F32)
            for c in range(channels):
                state_rows[row, c : c + 1, :] = state_ref[c, i, k : k + 1, :]
                grad_rows[row, c : c + 1, :] = DT_STEP * adj_rows[c, row : row + 1, :]
    w_in = w_in_ref[...]
    w_high = rounded(w_in)
    w_low = rounded(w_in - w_high)
    b_in = b_in_ref[...]
    b_high = rounded(b_in)
    b_next = rounded(b_in - b_high)
    b_last = rounded(b_in - b_high - b_next)
    joint_rows = jnp.concatenate(
        [w_high, b_high, b_next, b_last, w_high, jnp.zeros((8 - channels, hidden), F32)]
        + [w_low, jnp.zeros((16 - channels, hidden), F32)],
        axis=0,
    )
    w_first[...] = (0.5 * joint_rows).T.astype(BF16)
    w_back[...] = joint_rows[8:24].astype(BF16)
    w_mid = 0.5 * w_mid_ref[...].astype(F32)
    w_mid_half[...] = w_mid.astype(BF16)
    w_mid_t[...] = w_mid.T.astype(BF16)
    w_out_half[...] = jnp.concatenate(
        [0.5 * w_out_ref[...].astype(F32), jnp.zeros((16 - channels, hidden), F32)], axis=0
    ).T.astype(BF16)
    bias = jnp.broadcast_to(0.5 * b_mid_ref[...], (128, hidden)).T
    bias_mid[...] = bias
    totals[...] = jnp.zeros_like(totals)
    totals_in[...] = jnp.zeros_like(totals_in)
    totals_out[...] = jnp.zeros_like(totals_out)

    whole = norm_all.at[pl.ds(0, count - 1)]
    pltpu.make_async_copy(whole, whole, norm_sems.at[0]).wait()
    pltpu.make_async_copy(whole, whole, norm_sems.at[1]).wait()
    sum_squares = norm_mine[...] + jnp.sum(norm_all[0 : count - 1], axis=0)
    sum_squares = jnp.sum(sum_squares, axis=1, keepdims=True)
    entry_count = channels * columns * line * count
    inv_norm = lax.rsqrt(sum_squares / entry_count + EPS)
    row_index = lax.broadcasted_iota(jnp.int32, (8, line), 0)
    scale = jnp.where(row_index < channels, jnp.broadcast_to(inv_norm, (8, line)), 1.0)

    joints = (joint_even, joint_odd)
    slopes = (slope_even, slope_odd)
    deltas = (delta_even, delta_odd)

    def first_layer(row, turn, slot):
        scaled = state_rows[row] * scale
        high = rounded(scaled)
        low = scaled - high
        inputs = jnp.concatenate([high, low, high, jnp.zeros_like(high)], axis=0).astype(BF16)
        joints[slot][turn, hidden:, :] = inputs
        pre = nn_dot(w_first[...], inputs)
        bend = jnp.tanh(pre)
        gate = 1.0 + bend
        act = pre * gate
        slopes[slot][turn] = gate + act * (1.0 - bend)
        hidden_one = act.astype(BF16)
        joints[slot][turn, :hidden, :] = hidden_one
        return hidden_one

    def second_layer(row, hidden_one):
        pre = nn_dot(w_mid_t[...], hidden_one)
        pre = pre + jnp.concatenate([bias_mid[...]] * (line // 128), axis=1)
        bend = jnp.tanh(pre)
        gate = 1.0 + bend
        act = pre * gate
        slope_two = gate + act * (1.0 - bend)
        return act.astype(BF16), slope_two

    def last_layer(row, turn, slot, hidden_two, slope_two):
        out_grad = grad_rows[row].astype(BF16)
        back_two = nn_dot(w_out_half[...], out_grad)
        delta_two = (back_two * slope_two).astype(BF16)
        deltas[slot][turn] = delta_two
        return nt_dot(out_grad, hidden_two), nt_dot(joints[slot][turn], delta_two)

    def forward(turn, carry):
        ones = [first_layer(2 * turn + slot, turn, slot) for slot in range(2)]
        twos = [second_layer(2 * turn + slot, ones[slot]) for slot in range(2)]
        sums = [last_layer(2 * turn + slot, turn, slot, *twos[slot]) for slot in range(2)]
        totals_out[...] += sums[0][0] + sums[1][0]
        totals[...] += sums[0][1] + sums[1][1]
        return carry

    turns = columns // 2
    lax.fori_loop(0, turns, forward, 0)

    def backward(turn, carry):
        sums = []
        for slot in range(2):
            delta_one = nn_dot(w_mid_half[...], deltas[slot][turn]) * slopes[slot][turn]
            delta_one = delta_one.astype(BF16)
            sums.append(nt_dot(joints[slot][turn, hidden:, :], delta_one))
            back = nn_dot(w_back[...], delta_one)
            back = back[:8] + back[8:]
            for c in range(channels):
                back_rows[c, pl.ds(2 * turn + slot, 1), :] = back[c : c + 1, :]
        totals_in[...] += sums[0] + sums[1]
        return carry

    def plane_peer(d):
        to = lax.rem(my_plane + d, n_plane)
        return to, (to // 2, level * 4 + lax.rem(to, 2) * 2 + core)

    def line_peer(d):
        return (my_x, lax.rem(level + d, n_line) * 4 + side * 2 + core)

    def remote(src, dst, send_sem, recv_sem, to):
        copy = pltpu.make_async_remote_copy(
            src_ref=src,
            dst_ref=dst,
            send_sem=send_sem,
            recv_sem=recv_sem,
            device_id=to,
            device_id_type=MESH,
        )
        copy.start()
        return copy

    def ordered_sum(ref, size):
        return sum((ref[q] for q in range(1, size)), ref[0])

    for h in range(2):
        core_send[h] = totals[0:hidden, h * half : (h + 1) * half]
    core_copy = remote(
        core_send.at[1 - core], core_recv, core_sems.at[0], core_sems.at[1], other_core
    )
    lax.fori_loop(0, turns // 2, backward, 0)

    core_copy.wait()
    for q in range(n_plane):
        rows = slice(q * part, (q + 1) * part)
        plane_send[q] = core_send[core, rows, :] + core_recv[rows, :]
    plane_copies = []
    for d in range(1, n_plane):
        to, device = plane_peer(d)
        plane_copies.append(
            remote(
                plane_send.at[to],
                plane_all.at[my_plane],
                plane_send_sems.at[d],
                plane_recv_sems.at[d],
                device,
            )
        )
    plane_all[my_plane] = plane_send[my_plane]
    lax.fori_loop(turns // 2, turns, backward, 0)

    top = lax.broadcasted_iota(jnp.int32, (8, hidden), 0)
    mixed = jnp.where(
        top == channels + 1, totals[hidden : hidden + 8], totals_in[0:8] + totals_in[8:16]
    )
    for h in range(2):
        lanes = slice(h * half, (h + 1) * half)
        ext_core_send[h, 0:8, :] = mixed[:, lanes]
        ext_core_send[h, 8:16, :] = totals_out[0:8, lanes]
    ext_core_copy = remote(
        ext_core_send.at[1 - core],
        ext_core_recv,
        ext_core_sems.at[0],
        ext_core_sems.at[1],
        other_core,
    )

    for copy in plane_copies:
        copy.wait()
    line_send[...] = ordered_sum(plane_all, n_plane)
    line_copies = [
        remote(
            line_send,
            line_all.at[level],
            line_send_sems.at[d],
            line_recv_sems.at[d],
            line_peer(d),
        )
        for d in range(1, n_line)
    ]
    line_all[level] = line_send[...]

    ext_core_copy.wait()
    ext_plane_send[...] = ext_core_send[core] + ext_core_recv[...]
    ext_plane_copies = [
        remote(
            ext_plane_send,
            ext_plane_all.at[my_plane],
            ext_plane_send_sems.at[d],
            ext_plane_recv_sems.at[d],
            plane_peer(d)[1],
        )
        for d in range(1, n_plane)
    ]
    ext_plane_all[my_plane] = ext_plane_send[...]

    for copy in halo_copies:
        copy.wait()
    for c in range(channels):
        low_x[c, 0:z_elems, :] = x_halo[0, c]
        up_x[c, columns - z_elems : columns, :] = x_halo[1, c]
        if x_elems > 1:
            low_x[c, z_elems:columns, :] = adj_rows[c, 0 : columns - z_elems, :]
            up_x[c, 0 : columns - z_elems, :] = adj_rows[c, z_elems:columns, :]
        for i in range(x_elems):
            first, last = i * z_elems, (i + 1) * z_elems
            low_z[c, first : first + 1, :] = z_halo[0, c * x_elems + i]
            up_z[c, last - 1 : last, :] = z_halo[1, c * x_elems + i]
            if z_elems > 1:
                low_z[c, first + 1 : last, :] = adj_rows[c, first : last - 1, :]
                up_z[c, first : last - 1, :] = adj_rows[c, first + 1 : last, :]
    lane = lax.broadcasted_iota(jnp.int32, (columns, line), 1)
    row = lax.broadcasted_iota(jnp.int32, (columns, line), 0)
    spot_a, spot_b, spot_c, spot_j = (lane >> 4) & 3, (lane >> 2) & 3, lane & 3, lane >> 6
    bottom = jnp.zeros((columns, line), F32)
    ceiling = jnp.zeros((columns, line), F32)
    for i in range(x_elems):
        for k in range(z_elems):
            here = row == i * z_elems + k
            bottom = jnp.where(here, -2.0 * tags_ref[0, i, k].astype(F32), bottom)
            ceiling = jnp.where(here, -2.0 * tags_ref[1, i, k].astype(F32), ceiling)
    for c in range(channels):
        own = adj_rows[c]
        low_y = jnp.where(spot_j == 0, bottom * own, pltpu.roll(own, 52, 1) - own)
        up_y = jnp.where(
            spot_j == line // 64 - 1, ceiling * own, pltpu.roll(own, line - 52, 1) - own
        )
        jump = (
            jnp.where(spot_a == 0, pltpu.roll(low_x[c], line - 48, 1) - own, 0.0)
            + jnp.where(spot_a == 3, pltpu.roll(up_x[c], 48, 1) - own, 0.0)
            + jnp.where(spot_b == 0, low_y, 0.0)
            + jnp.where(spot_b == 3, up_y, 0.0)
            + jnp.where(spot_c == 0, pltpu.roll(low_z[c], line - 3, 1) - own, 0.0)
            + jnp.where(spot_c == 3, pltpu.roll(up_z[c], 3, 1) - own, 0.0)
        )
        back_rows[c] = own + 0.5 * KAPPA * jump + inv_norm * back_rows[c]
        for i in range(x_elems):
            gstate_ref[c, i] = back_rows[c, i * z_elems : (i + 1) * z_elems, :]
    stores = []

    def store(src, dst):
        copy = pltpu.make_async_copy(src, dst, store_sems.at[len(stores)])
        copy.start()
        stores.append(copy)

    def store_part(h, q):
        dst = gmid_hbm.at[
            pl.ds(pl.multiple_of(q * part, part), part),
            pl.ds(pl.multiple_of(h * half, half), half),
        ]
        store(gathered.at[h, q], dst)

    store(gstate_ref, gstate_hbm)

    for copy in ext_plane_copies:
        copy.wait()
    ext_line_send[...] = ordered_sum(ext_plane_all, n_plane)
    ext_line_copies = [
        remote(
            ext_line_send,
            ext_line_all.at[level],
            ext_line_send_sems.at[d],
            ext_line_recv_sems.at[d],
            line_peer(d),
        )
        for d in range(1, n_line)
    ]
    ext_line_all[level] = ext_line_send[...]

    def to_pair(slot, d):
        return remote(
            gathered.at[core, slot],
            gathered.at[core, slot],
            pair_send_sems.at[d],
            pair_recv_sems.at[d],
            other_core,
        )

    factor = 4.0 / math.sqrt(entry_count // channels)
    for copy in line_copies:
        copy.wait()
    gathered[core, my_plane] = factor * ordered_sum(line_all, n_line)
    spread_copies = [
        remote(
            gathered.at[core, my_plane],
            gathered.at[core, my_plane],
            spread_send_sems.at[d],
            spread_recv_sems.at[d],
            plane_peer(d)[1],
        )
        for d in range(1, n_plane)
    ]
    pair_copies = [to_pair(my_plane, 0)]
    store_part(core, my_plane)
    for copy in ext_line_copies:
        copy.wait()
    gathered_ext[core] = factor * ordered_sum(ext_line_all, n_line)
    ext_pair_copy = remote(
        gathered_ext.at[core],
        gathered_ext.at[core],
        pair_send_sems.at[n_plane],
        pair_recv_sems.at[n_plane],
        other_core,
    )
    for d in range(1, n_plane):
        spread_copies[d - 1].wait_recv()
        slot = lax.rem(my_plane + n_plane - d, n_plane)
        pair_copies.append(to_pair(slot, d))
        store_part(core, slot)
    ext_pair_copy.wait()
    for h in range(2):
        lanes = slice(h * half, (h + 1) * half)
        gin_ref[:, lanes] = gathered_ext[h, 0:channels]
        gbin_ref[:, lanes] = gathered_ext[h, channels : channels + 1]
        gbmid_ref[:, lanes] = gathered_ext[h, channels + 1 : channels + 2]
        gout_ref[:, lanes] = gathered_ext[h, 8 : 8 + channels]
    store(gin_ref, gin_hbm)
    store(gbin_ref, gbin_hbm)
    store(gbmid_ref, gbmid_hbm)
    store(gout_ref, gout_hbm)
    for d in range(n_plane):
        pair_copies[d].wait()
        store_part(1 - core, lax.rem(my_plane + n_plane - d, n_plane))
    for copy in spread_copies:
        copy.wait_send()
    for copy in stores:
        copy.wait()


def writer(*refs):
    half = len(refs) // 2
    copies = [
        pltpu.make_async_copy(src, dst, refs[-1].at[spot])
        for spot, (src, dst) in enumerate(zip(refs[:half], refs[half:-1]))
    ]
    for copy in copies:
        copy.start()
    for copy in copies:
        copy.wait()


def per_device(dims, state, cotangent, local_inverse, wall_tags, w_in, b_in, w_mid, b_mid, w_out):
    gx, gz = dims
    channels, x_elems, z_elems, line = state.shape
    hidden = w_mid.shape[0]
    columns = x_elems * z_elems
    n_plane, n_line = gx * 2, gz // 4
    part = hidden // n_plane
    half = hidden // 2
    turns = columns // 2
    vmem = pl.BlockSpec(memory_space=pltpu.VMEM)
    hbm = pl.BlockSpec(memory_space=pltpu.HBM)
    rows = pltpu.VMEM((channels, columns, line), F32)
    dma = pltpu.SemaphoreType.DMA

    def same(array):
        return pltpu.VMEM(array.shape, array.dtype)

    b_in, b_mid = b_in.reshape(1, hidden), b_mid.reshape(1, hidden)
    out_shape = (
        jax.ShapeDtypeStruct(state.shape, F32),
        jax.ShapeDtypeStruct((channels, hidden), F32),
        jax.ShapeDtypeStruct((1, hidden), F32),
        jax.ShapeDtypeStruct((hidden, hidden), F32),
        jax.ShapeDtypeStruct((1, hidden), F32),
        jax.ShapeDtypeStruct((channels, hidden), F32),
    )
    out = pl.pallas_call(
        functools.partial(kernel, dims),
        out_shape=out_shape,
        in_specs=[hbm] * 8 + [vmem],
        out_specs=(hbm,) * 6,
        scratch_shapes=[
            same(state),
            pltpu.VMEM((channels, hidden), F32),
            pltpu.VMEM((1, hidden), F32),
            pltpu.VMEM((1, hidden), F32),
            pltpu.VMEM((channels, hidden), F32),
            pltpu.VMEM((2, n_plane, part, half), F32),
            pltpu.VMEM((2, 16, half), F32),
            same(state),
            same(cotangent),
            same(local_inverse),
            pltpu.SMEM(wall_tags.shape, jnp.int32),
            same(w_in),
            same(b_in),
            same(w_mid),
            same(b_mid),
            pltpu.VMEM((columns, 8, line), F32),
            pltpu.VMEM((columns, 16, line), F32),
            rows,
            rows,
            rows,
            rows,
            rows,
            rows,
            pltpu.VMEM((2, channels, z_elems, line), F32),
            pltpu.VMEM((2, channels, z_elems, line), F32),
            pltpu.VMEM((2, channels * x_elems, 1, line), F32),
            pltpu.VMEM((2, channels * x_elems, 1, line), F32),
            pltpu.VMEM((hidden, 32), BF16),
            pltpu.VMEM((16, hidden), BF16),
            pltpu.VMEM((hidden, hidden), BF16),
            pltpu.VMEM((hidden, hidden), BF16),
            pltpu.VMEM((hidden, 16), BF16),
            pltpu.VMEM((hidden, 128), F32),
            pltpu.VMEM((turns, hidden + 32, line), BF16),
            pltpu.VMEM((turns, hidden + 32, line), BF16),
            pltpu.VMEM((turns, hidden, line), F32),
            pltpu.VMEM((turns, hidden, line), F32),
            pltpu.VMEM((turns, hidden, line), BF16),
            pltpu.VMEM((turns, hidden, line), BF16),
            pltpu.VMEM((hidden + 32, hidden), F32),
            pltpu.VMEM((32, hidden), F32),
            pltpu.VMEM((16, hidden), F32),
            pltpu.VMEM((1, 128), F32),
            pltpu.VMEM((gx * gz, 1, 128), F32),
            pltpu.VMEM((2, hidden, half), F32),
            pltpu.VMEM((hidden, half), F32),
            pltpu.VMEM((n_plane, part, half), F32),
            pltpu.VMEM((n_plane, part, half), F32),
            pltpu.VMEM((part, half), F32),
            pltpu.VMEM((n_line, part, half), F32),
            pltpu.VMEM((2, 16, half), F32),
            pltpu.VMEM((16, half), F32),
            pltpu.VMEM((16, half), F32),
            pltpu.VMEM((n_plane, 16, half), F32),
            pltpu.VMEM((16, half), F32),
            pltpu.VMEM((n_line, 16, half), F32),
            dma((11,)),
            dma((2 * n_plane + 5,)),
            dma((2,)),
            dma((4,)),
            dma((4,)),
            dma((2,)),
            dma((n_plane,)),
            dma((n_plane,)),
            dma((n_line,)),
            dma((n_line,)),
            dma((2,)),
            dma((n_plane,)),
            dma((n_plane,)),
            dma((n_line,)),
            dma((n_line,)),
            dma((n_plane,)),
            dma((n_plane,)),
            dma((n_plane + 1,)),
            dma((n_plane + 1,)),
        ],
        compiler_params=pltpu.CompilerParams(
            collective_id=0, has_side_effects=True, vmem_limit_bytes=62 * 1024 * 1024
        ),
    )(state, cotangent, local_inverse, wall_tags, w_in, b_in, w_mid, b_mid, w_out.T)
    out = pl.pallas_call(
        writer,
        out_shape=out_shape,
        in_specs=[hbm] * 6,
        out_specs=(hbm,) * 6,
        scratch_shapes=[dma((6,))],
        compiler_params=pltpu.CompilerParams(vmem_limit_bytes=62 * 1024 * 1024),
    )(*out)
    return out[0], out[1], out[2].reshape(hidden), out[3], out[4].reshape(hidden), out[5].T


def solution(mesh):
    placed = (
        P(None, "gx", "gz", None),
        P(None, "gx", "gz", None),
        P(None, "gx", "gz", None),
        P(None, "gx", "gz"),
        P(),
        P(),
        P(),
        P(),
        P(),
    )
    return jax.shard_map(
        functools.partial(per_device, (mesh.shape["gx"], mesh.shape["gz"])),
        mesh=mesh,
        in_specs=placed,
        out_specs=(P(None, "gx", "gz", None), P(), P(), P(), P(), P()),
        check_vma=False,
    )
```

time: 45.2 us -> 44.4 us (0.982)
  local copies, waits for them, and re-layouts: 8.5 us -> 0 us
  Pallas kernels: 35.7 us -> 43.6 us
    unnamed x23 -> x0, local copies, waits for them, and re-layouts: 8.5 us -> none
    pallas_call x1 -> x2, Pallas kernels: 35.7 us -> 43.6 us  [the longest x1 31.5 us: per_device(): pl.pallas_call(functools.partial(kernel, dims), out_shape=out_shape, in_s...]
where the time goes in v2:
time: 44.4 us; the launch traced here: 44.2 us
  Pallas kernels  43.6 us (98%)
  between operations  0.64 us (1%)
    pallas_call x1, Pallas kernels, per_device(): pl.pallas_call(functools.partial(kernel, dims), out_shape=out_shape, in_s...  31.5 us
    pallas_call x1, Pallas kernels, per_device(): pl.pallas_call(writer, out_shape=out_shape, in_specs=[hbm] * 6, out_specs...  12.1 us

profile of v2, /device:TPU:0, one launch (start us, length us, event | category | flops | bytes accessed | tf_op | source)
XLA Modules:
  0.0 44.2 jit_solution(11967945129709167300)
XLA Ops:
  0.6 31.5 %shard_map.136 = (f32[5,2,4,512]{3,2,1,0:T(4,128)}, f32[5,256]{1,0:T(8,128)}, f32[1,256]{1,0:T(1,128)}, f32[256,256]{1,0:T(8,128)}, f32[1,256]{1,0:T(1,128)}, /*index=5*/f32[5,256]{1,0:T(8,128)}) custom-call(f32[5,2,4,512]{3,2,1,0:T(4,128)} %state_hbm.1, f32[5,2,4,512]{3,2,1,0:T(4,128)} %cot_hbm.1, f32[64,2,4,512]{3,2,1,0:T(4,128)} %inv_hbm.1, ...), custom_call_target="tpu_custom_call" | custom-call | tf_op jit(solution)/shard_map/pallas_call | solution.py:629
  32.1 12.1 %shard_map.137 = (f32[5,2,4,512]{3,2,1,0:T(4,128)}, f32[5,256]{1,0:T(8,128)}, f32[1,256]{1,0:T(1,128)}, f32[256,256]{1,0:T(8,128)}, f32[1,256]{1,0:T(1,128)}, /*index=5*/f32[5,256]{1,0:T(8,128)}) custom-call(f32[5,2,4,512]{3,2,1,0:T(4,128)} %get-tuple-element.18.refs_0_, f32[5,256]{1,0:T(8,128)} %get-tuple-element.19.refs_1_, ...), custom_call_target="tpu_custom_call" | custom-call | tf_op jit(solution)/shard_map/pallas_call | solution.py:715

commit v3 on v2

--- a/solution.py
+++ b/solution.py
@@ -80,12 +80,9 @@
     w_mid_half,
     w_out_half,
     bias_mid,
-    joint_even,
-    joint_odd,
-    slope_even,
-    slope_odd,
-    delta_even,
-    delta_odd,
+    joints,
+    slopes,
+    deltas,
     totals,
     totals_in,
     totals_out,
@@ -162,7 +159,7 @@
         )
         for p in range(pieces)
     ]
-    for load in loads[:2] + inv_loads + loads[2:]:
+    for load in loads[2:] + loads[:2] + inv_loads:
         load.start()
 
     barrier = pltpu.get_barrier_semaphore()
@@ -175,6 +172,34 @@
         return carry
 
     lax.fori_loop(1, count, greet, 0)
+
+    for load in loads[2:]:
+        load.wait()
+    w_in = w_in_ref[...]
+    w_high = rounded(w_in)
+    w_low = rounded(w_in - w_high)
+    b_in = b_in_ref[...]
+    b_high = rounded(b_in)
+    b_next = rounded(b_in - b_high)
+    b_last = rounded(b_in - b_high - b_next)
+    joint_rows = jnp.concatenate(
+        [w_high, b_high, b_next, b_last, w_high, jnp.zeros((8 - channels, hidden), F32)]
+        + [w_low, jnp.zeros((16 - channels, hidden), F32)],
+        axis=0,
+    )
+    w_first[...] = (0.5 * joint_rows).T.astype(BF16)
+    w_back[...] = joint_rows[8:24].astype(BF16)
+    w_mid = 0.5 * w_mid_ref[...].astype(F32)
+    w_mid_half[...] = w_mid.astype(BF16)
+    w_mid_t[...] = w_mid.T.astype(BF16)
+    w_out_half[...] = jnp.concatenate(
+        [0.5 * w_out_ref[...].astype(F32), jnp.zeros((16 - channels, hidden), F32)], axis=0
+    ).T.astype(BF16)
+    bias = jnp.broadcast_to(0.5 * b_mid_ref[...], (128, hidden)).T
+    bias_mid[...] = bias
+    totals[...] = jnp.zeros_like(totals)
+    totals_in[...] = jnp.zeros_like(totals_in)
+    totals_out[...] = jnp.zeros_like(totals_out)
 
     loads[0].wait()
     squares = state_ref[...] * state_ref[...]
@@ -224,7 +249,7 @@
     sums = (jnp.zeros((columns, 128), F32),) * (channels * blocks)
     for p in range(pieces):
         inv_loads[p].wait()
-        sums = lax.fori_loop(p * piece, (p + 1) * piece, adjoint_step, sums, unroll=4)
+        sums = lax.fori_loop(p * piece, (p + 1) * piece, adjoint_step, sums, unroll=piece)
     for c in range(channels):
         for t in range(blocks):
             adj_rows[c, :, t * 128 : (t + 1) * 128] = sums[c * blocks + t]
@@ -257,8 +282,6 @@
         copy.start()
         halo_copies.append(copy)
 
-    for load in loads[2:]:
-        load.wait()
     for i in range(x_elems):
         for k in range(z_elems):
             row = i * z_elems + k
@@ -267,32 +290,6 @@
             for c in range(channels):
                 state_rows[row, c : c + 1, :] = state_ref[c, i, k : k + 1, :]
                 grad_rows[row, c : c + 1, :] = DT_STEP * adj_rows[c, row : row + 1, :]
-    w_in = w_in_ref[...]
-    w_high = rounded(w_in)
-    w_low = rounded(w_in - w_high)
-    b_in = b_in_ref[...]
-    b_high = rounded(b_in)
-    b_next = rounded(b_in - b_high)
-    b_last = rounded(b_in - b_high - b_next)
-    joint_rows = jnp.concatenate(
-        [w_high, b_high, b_next, b_last, w_high, jnp.zeros((8 - channels, hidden), F32)]
-        + [w_low, jnp.zeros((16 - channels, hidden), F32)],
-        axis=0,
-    )
-    w_first[...] = (0.5 * joint_rows).T.astype(BF16)
-    w_back[...] = joint_rows[8:24].astype(BF16)
-    w_mid = 0.5 * w_mid_ref[...].astype(F32)
-    w_mid_half[...] = w_mid.astype(BF16)
-    w_mid_t[...] = w_mid.T.astype(BF16)
-    w_out_half[...] = jnp.concatenate(
-        [0.5 * w_out_ref[...].astype(F32), jnp.zeros((16 - channels, hidden), F32)], axis=0
-    ).T.astype(BF16)
-    bias = jnp.broadcast_to(0.5 * b_mid_ref[...], (128, hidden)).T
-    bias_mid[...] = bias
-    totals[...] = jnp.zeros_like(totals)
-    totals_in[...] = jnp.zeros_like(totals_in)
-    totals_out[...] = jnp.zeros_like(totals_out)
-
     whole = norm_all.at[pl.ds(0, count - 1)]
     pltpu.make_async_copy(whole, whole, norm_sems.at[0]).wait()
     pltpu.make_async_copy(whole, whole, norm_sems.at[1]).wait()
@@ -303,64 +300,50 @@
     row_index = lax.broadcasted_iota(jnp.int32, (8, line), 0)
     scale = jnp.where(row_index < channels, jnp.broadcast_to(inv_norm, (8, line)), 1.0)
 
-    joints = (joint_even, joint_odd)
-    slopes = (slope_even, slope_odd)
-    deltas = (delta_even, delta_odd)
-
-    def first_layer(row, turn, slot):
+    def first_layer(row):
         scaled = state_rows[row] * scale
         high = rounded(scaled)
         low = scaled - high
         inputs = jnp.concatenate([high, low, high, jnp.zeros_like(high)], axis=0).astype(BF16)
-        joints[slot][turn, hidden:, :] = inputs
+        joints[row, hidden:, :] = inputs
         pre = nn_dot(w_first[...], inputs)
         bend = jnp.tanh(pre)
         gate = 1.0 + bend
         act = pre * gate
-        slopes[slot][turn] = gate + act * (1.0 - bend)
-        hidden_one = act.astype(BF16)
-        joints[slot][turn, :hidden, :] = hidden_one
-        return hidden_one
-
-    def second_layer(row, hidden_one):
-        pre = nn_dot(w_mid_t[...], hidden_one)
+        slopes[row] = gate + act * (1.0 - bend)
+        joints[row, :hidden, :] = act.astype(BF16)
+
+    def second_layer(row):
+        pre = nn_dot(w_mid_t[...], joints[row, :hidden, :])
         pre = pre + jnp.concatenate([bias_mid[...]] * (line // 128), axis=1)
         bend = jnp.tanh(pre)
         gate = 1.0 + bend
         act = pre * gate
         slope_two = gate + act * (1.0 - bend)
-        return act.astype(BF16), slope_two
-
-    def last_layer(row, turn, slot, hidden_two, slope_two):
         out_grad = grad_rows[row].astype(BF16)
+        totals_out[...] += nt_dot(out_grad, act.astype(BF16))
         back_two = nn_dot(w_out_half[...], out_grad)
-        delta_two = (back_two * slope_two).astype(BF16)
-        deltas[slot][turn] = delta_two
-        return nt_dot(out_grad, hidden_two), nt_dot(joints[slot][turn], delta_two)
-
-    def forward(turn, carry):
-        ones = [first_layer(2 * turn + slot, turn, slot) for slot in range(2)]
-        twos = [second_layer(2 * turn + slot, ones[slot]) for slot in range(2)]
-        sums = [last_layer(2 * turn + slot, turn, slot, *twos[slot]) for slot in range(2)]
-        totals_out[...] += sums[0][0] + sums[1][0]
-        totals[...] += sums[0][1] + sums[1][1]
-        return carry
-
-    turns = columns // 2
-    lax.fori_loop(0, turns, forward, 0)
-
-    def backward(turn, carry):
-        sums = []
-        for slot in range(2):
-            delta_one = nn_dot(w_mid_half[...], deltas[slot][turn]) * slopes[slot][turn]
-            delta_one = delta_one.astype(BF16)
-            sums.append(nt_dot(joints[slot][turn, hidden:, :], delta_one))
-            back = nn_dot(w_back[...], delta_one)
-            back = back[:8] + back[8:]
-            for c in range(channels):
-                back_rows[c, pl.ds(2 * turn + slot, 1), :] = back[c : c + 1, :]
-        totals_in[...] += sums[0] + sums[1]
-        return carry
+        deltas[row] = (back_two * slope_two).astype(BF16)
+
+    def last_layer(row):
+        totals[...] += nt_dot(joints[row], deltas[row])
+
+    for step in range(columns + 2):
+        if step < columns:
+            first_layer(step)
+        if 1 <= step <= columns:
+            second_layer(step - 1)
+        if step >= 2:
+            last_layer(step - 2)
+
+    def backward(row):
+        delta_one = nn_dot(w_mid_half[...], deltas[row]) * slopes[row]
+        delta_one = delta_one.astype(BF16)
+        totals_in[...] += nt_dot(joints[row, hidden:, :], delta_one)
+        back = nn_dot(w_back[...], delta_one)
+        back = back[:8] + back[8:]
+        for c in range(channels):
+            back_rows[c, row : row + 1, :] = back[c : c + 1, :]
 
     def plane_peer(d):
         to = lax.rem(my_plane + d, n_plane)
@@ -389,7 +372,8 @@
     core_copy = remote(
         core_send.at[1 - core], core_recv, core_sems.at[0], core_sems.at[1], other_core
     )
-    lax.fori_loop(0, turns // 2, backward, 0)
+    for row in range(columns // 2):
+        backward(row)
 
     core_copy.wait()
     for q in range(n_plane):
@@ -408,7 +392,8 @@
             )
         )
     plane_all[my_plane] = plane_send[my_plane]
-    lax.fori_loop(turns // 2, turns, backward, 0)
+    for row in range(columns // 2, columns):
+        backward(row)
 
     top = lax.broadcasted_iota(jnp.int32, (8, hidden), 0)
     mixed = jnp.where(
@@ -589,15 +574,23 @@
 
 
 def writer(*refs):
-    half = len(refs) // 2
-    copies = [
-        pltpu.make_async_copy(src, dst, refs[-1].at[spot])
-        for spot, (src, dst) in enumerate(zip(refs[:half], refs[half:-1]))
+    size = (len(refs) - 1) // 3
+    sems = refs[-1]
+    sources, results, held = refs[:size], refs[size : 2 * size], refs[2 * size : -1]
+    loads = [
+        pltpu.make_async_copy(sources[spot], held[spot], sems.at[spot]) for spot in range(size)
     ]
-    for copy in copies:
-        copy.start()
-    for copy in copies:
-        copy.wait()
+    stores = [
+        pltpu.make_async_copy(held[spot], results[spot], sems.at[size + spot])
+        for spot in range(size)
+    ]
+    for load in loads:
+        load.start()
+    for load, store in zip(loads, stores):
+        load.wait()
+        store.start()
+    for store in stores:
+        store.wait()
 
 
 def per_device(dims, state, cotangent, local_inverse, wall_tags, w_in, b_in, w_mid, b_mid, w_out):
@@ -608,7 +601,6 @@
     n_plane, n_line = gx * 2, gz // 4
     part = hidden // n_plane
     half = hidden // 2
-    turns = columns // 2
     vmem = pl.BlockSpec(memory_space=pltpu.VMEM)
     hbm = pl.BlockSpec(memory_space=pltpu.HBM)
     rows = pltpu.VMEM((channels, columns, line), F32)
@@ -665,12 +657,9 @@
             pltpu.VMEM((hidden, hidden), BF16),
             pltpu.VMEM((hidden, 16), BF16),
             pltpu.VMEM((hidden, 128), F32),
-            pltpu.VMEM((turns, hidden + 32, line), BF16),
-            pltpu.VMEM((turns, hidden + 32, line), BF16),
-            pltpu.VMEM((turns, hidden, line), F32),
-            pltpu.VMEM((turns, hidden, line), F32),
-            pltpu.VMEM((turns, hidden, line), BF16),
-            pltpu.VMEM((turns, hidden, line), BF16),
+            pltpu.VMEM((columns, hidden + 32, line), BF16),
+            pltpu.VMEM((columns, hidden, line), F32),
+            pltpu.VMEM((columns, hidden, line), BF16),
             pltpu.VMEM((hidden + 32, hidden), F32),
             pltpu.VMEM((32, hidden), F32),
             pltpu.VMEM((16, hidden), F32),
@@ -717,7 +706,7 @@
         out_shape=out_shape,
         in_specs=[hbm] * 6,
         out_specs=(hbm,) * 6,
-        scratch_shapes=[dma((6,))],
+        scratch_shapes=[pltpu.VMEM(o.shape, F32) for o in out_shape] + [dma((12,))],
         compiler_params=pltpu.CompilerParams(vmem_limit_bytes=62 * 1024 * 1024),
     )(*out)
     return out[0], out[1], out[2].reshape(hidden), out[3], out[4].reshape(hidden), out[5].T

time: 44.4 us -> 33 us (0.74)
  Pallas kernels: 43.6 us -> 32.1 us
    pallas_call x1, Pallas kernels: 12.1 us -> 1.83 us  [per_device(): pl.pallas_call(writer, out_shape=out_shape, in_specs=[hbm] * 6, out_specs...]
    pallas_call x1, Pallas kernels: 31.5 us -> 30.3 us  [per_device(): pl.pallas_call(functools.partial(kernel, dims), out_shape=out_shape, in_s...]
where the time goes in v3:
time: 33 us; the launch traced here: 32.7 us
  Pallas kernels  32.1 us (97%)
  between operations  0.64 us (2%)
    pallas_call x1, Pallas kernels, per_device(): pl.pallas_call(functools.partial(kernel, dims), out_shape=out_shape, in_s...  30.3 us
    pallas_call x1, Pallas kernels, per_device(): pl.pallas_call(writer, out_shape=out_shape, in_specs=[hbm] * 6, out_specs...  1.83 us

profile of v3, /device:TPU:0, one launch (start us, length us, event | category | flops | bytes accessed | tf_op | source)
XLA Modules:
  0.0 32.7 jit_solution(14974440921104379084)
XLA Ops:
  0.6 30.3 %shard_map.136 = (f32[5,2,4,512]{3,2,1,0:T(4,128)}, f32[5,256]{1,0:T(8,128)}, f32[1,256]{1,0:T(1,128)}, f32[256,256]{1,0:T(8,128)}, f32[1,256]{1,0:T(1,128)}, /*index=5*/f32[5,256]{1,0:T(8,128)}) custom-call(f32[5,2,4,512]{3,2,1,0:T(4,128)} %state_hbm.1, f32[5,2,4,512]{3,2,1,0:T(4,128)} %cot_hbm.1, f32[64,2,4,512]{3,2,1,0:T(4,128)} %inv_hbm.1, ...), custom_call_target="tpu_custom_call" | custom-call | tf_op jit(solution)/shard_map/pallas_call | solution.py:621
  30.9 1.8 %shard_map.137 = (f32[5,2,4,512]{3,2,1,0:T(4,128)}, f32[5,256]{1,0:T(8,128)}, f32[1,256]{1,0:T(1,128)}, f32[256,256]{1,0:T(8,128)}, f32[1,256]{1,0:T(1,128)}, /*index=5*/f32[5,256]{1,0:T(8,128)}) custom-call(f32[5,2,4,512]{3,2,1,0:T(4,128)} %get-tuple-element.18.refs_0_, f32[5,256]{1,0:T(8,128)} %get-tuple-element.19.refs_1_, ...), custom_call_target="tpu_custom_call" | custom-call | tf_op jit(solution)/shard_map/pallas_call | solution.py:704

commit v4 on v3

--- a/solution.py
+++ b/solution.py
@@ -81,13 +81,16 @@
     w_out_half,
     bias_mid,
     joints,
-    slopes,
+    bends,
+    hiddens,
     deltas,
     totals,
     totals_in,
     totals_out,
     norm_mine,
     norm_all,
+    norm_plane,
+    norm_line,
     core_send,
     core_recv,
     plane_send,
@@ -103,6 +106,7 @@
     load_sems,
     store_sems,
     norm_sems,
+    norm_line_sems,
     halo_send_sems,
     halo_recv_sems,
     core_sems,
@@ -164,14 +168,56 @@
 
     barrier = pltpu.get_barrier_semaphore()
 
-    def greet(step, carry):
-        to = lax.rem(me + step, count)
-        pl.semaphore_signal(
-            barrier, inc=1, device_id=(to // gz, lax.rem(to, gz)), device_id_type=MESH
-        )
-        return carry
-
-    lax.fori_loop(1, count, greet, 0)
+    def plane_peer(d):
+        to = lax.rem(my_plane + d, n_plane)
+        return to, (to // 2, level * 4 + lax.rem(to, 2) * 2 + core)
+
+    def line_peer(d):
+        return (my_x, lax.rem(level + d, n_line) * 4 + side * 2 + core)
+
+    def next_x(d):
+        return (lax.rem(my_x + gx + d, gx), my_z)
+
+    def next_z(d):
+        return (my_x, lax.rem(my_z + gz + d, gz))
+
+    plane_peers = [other_core]
+    for d in range(1, n_plane):
+        x, z = plane_peer(d)[1]
+        plane_peers += [(x, z), (x, z + 1 - 2 * core)]
+    line_peers = [line_peer(d) for d in range(1, n_line)]
+    friends = plane_peers + line_peers + [next_z(-1), next_z(1)]
+    for friend in friends:
+        pl.semaphore_signal(barrier, inc=1, device_id=friend, device_id_type=MESH)
+
+    loads[0].wait()
+    squares = state_ref[...] * state_ref[...]
+    squares = jnp.sum(jnp.sum(squares, axis=0), axis=0)
+    folded = squares[:, :128]
+    for start in range(128, line, 128):
+        folded = folded + squares[:, start : start + 128]
+    norm_mine[...] = jnp.sum(folded, axis=0, keepdims=True)
+
+    pl.semaphore_wait(barrier, len(friends))
+
+    def send_norm(source, slots, sems, peers):
+        for spot, peer in enumerate(peers):
+            pltpu.make_async_remote_copy(
+                src_ref=source,
+                dst_ref=slots.at[spot],
+                send_sem=sems.at[0],
+                recv_sem=sems.at[1],
+                device_id=peer,
+                device_id_type=MESH,
+            ).start()
+
+    def wait_norm(slots, sems, size):
+        whole = slots.at[pl.ds(0, size)]
+        pltpu.make_async_copy(whole, whole, sems.at[0]).wait()
+        pltpu.make_async_copy(whole, whole, sems.at[1]).wait()
+        return jnp.sum(slots[0:size], axis=0)
+
+    send_norm(norm_mine, norm_all, norm_sems, plane_peers)
 
     for load in loads[2:]:
         load.wait()
@@ -201,30 +247,6 @@
     totals_in[...] = jnp.zeros_like(totals_in)
     totals_out[...] = jnp.zeros_like(totals_out)
 
-    loads[0].wait()
-    squares = state_ref[...] * state_ref[...]
-    squares = jnp.sum(jnp.sum(squares, axis=0), axis=0)
-    folded = squares[:, :128]
-    for start in range(128, line, 128):
-        folded = folded + squares[:, start : start + 128]
-    norm_mine[...] = jnp.sum(folded, axis=0, keepdims=True)
-
-    pl.semaphore_wait(barrier, count - 1)
-
-    def send_norm(step, carry):
-        to = lax.rem(me + step, count)
-        pltpu.make_async_remote_copy(
-            src_ref=norm_mine,
-            dst_ref=norm_all.at[step - 1],
-            send_sem=norm_sems.at[0],
-            recv_sem=norm_sems.at[1],
-            device_id=(to // gz, lax.rem(to, gz)),
-            device_id_type=MESH,
-        ).start()
-        return carry
-
-    lax.fori_loop(1, count, send_norm, 0)
-
     loads[1].wait()
     for c in range(channels):
         for i in range(x_elems):
@@ -250,6 +272,9 @@
     for p in range(pieces):
         inv_loads[p].wait()
         sums = lax.fori_loop(p * piece, (p + 1) * piece, adjoint_step, sums, unroll=piece)
+        if p == 1:
+            norm_plane[...] = norm_mine[...] + wait_norm(norm_all, norm_sems, len(plane_peers))
+            send_norm(norm_plane, norm_line, norm_line_sems, line_peers)
     for c in range(channels):
         for t in range(blocks):
             adj_rows[c, :, t * 128 : (t + 1) * 128] = sums[c * blocks + t]
@@ -265,10 +290,10 @@
     halo_copies = []
     for spot, (src, dst, to) in enumerate(
         (
-            (x_send.at[0], x_halo.at[1], (lax.rem(my_x + gx - 1, gx), my_z)),
-            (x_send.at[1], x_halo.at[0], (lax.rem(my_x + 1, gx), my_z)),
-            (z_send.at[0], z_halo.at[1], (my_x, lax.rem(my_z + gz - 1, gz))),
-            (z_send.at[1], z_halo.at[0], (my_x, lax.rem(my_z + 1, gz))),
+            (x_send.at[0], x_halo.at[1], next_x(-1)),
+            (x_send.at[1], x_halo.at[0], next_x(1)),
+            (z_send.at[0], z_halo.at[1], next_z(-1)),
+            (z_send.at[1], z_halo.at[0], next_z(1)),
         )
     ):
         copy = pltpu.make_async_remote_copy(
@@ -290,10 +315,9 @@
             for c in range(channels):
                 state_rows[row, c : c + 1, :] = state_ref[c, i, k : k + 1, :]
                 grad_rows[row, c : c + 1, :] = DT_STEP * adj_rows[c, row : row + 1, :]
-    whole = norm_all.at[pl.ds(0, count - 1)]
-    pltpu.make_async_copy(whole, whole, norm_sems.at[0]).wait()
-    pltpu.make_async_copy(whole, whole, norm_sems.at[1]).wait()
-    sum_squares = norm_mine[...] + jnp.sum(norm_all[0 : count - 1], axis=0)
+    sum_squares = norm_plane[...]
+    if line_peers:
+        sum_squares = sum_squares + wait_norm(norm_line, norm_line_sems, len(line_peers))
     sum_squares = jnp.sum(sum_squares, axis=1, keepdims=True)
     entry_count = channels * columns * line * count
     inv_norm = lax.rsqrt(sum_squares / entry_count + EPS)
@@ -310,7 +334,7 @@
         bend = jnp.tanh(pre)
         gate = 1.0 + bend
         act = pre * gate
-        slopes[row] = gate + act * (1.0 - bend)
+        bends[row] = bend
         joints[row, :hidden, :] = act.astype(BF16)
 
     def second_layer(row):
@@ -321,7 +345,7 @@
         act = pre * gate
         slope_two = gate + act * (1.0 - bend)
         out_grad = grad_rows[row].astype(BF16)
-        totals_out[...] += nt_dot(out_grad, act.astype(BF16))
+        hiddens[row] = act.astype(BF16)
         back_two = nn_dot(w_out_half[...], out_grad)
         deltas[row] = (back_two * slope_two).astype(BF16)
 
@@ -337,20 +361,16 @@
             last_layer(step - 2)
 
     def backward(row):
-        delta_one = nn_dot(w_mid_half[...], deltas[row]) * slopes[row]
+        bend = bends[row]
+        slope = 1.0 + bend + joints[row, :hidden, :].astype(F32) * (1.0 - bend)
+        delta_one = nn_dot(w_mid_half[...], deltas[row]) * slope
         delta_one = delta_one.astype(BF16)
         totals_in[...] += nt_dot(joints[row, hidden:, :], delta_one)
+        totals_out[...] += nt_dot(grad_rows[row].astype(BF16), hiddens[row])
         back = nn_dot(w_back[...], delta_one)
         back = back[:8] + back[8:]
         for c in range(channels):
             back_rows[c, row : row + 1, :] = back[c : c + 1, :]
-
-    def plane_peer(d):
-        to = lax.rem(my_plane + d, n_plane)
-        return to, (to // 2, level * 4 + lax.rem(to, 2) * 2 + core)
-
-    def line_peer(d):
-        return (my_x, lax.rem(level + d, n_line) * 4 + side * 2 + core)
 
     def remote(src, dst, send_sem, recv_sem, to):
         copy = pltpu.make_async_remote_copy(
@@ -372,7 +392,8 @@
     core_copy = remote(
         core_send.at[1 - core], core_recv, core_sems.at[0], core_sems.at[1], other_core
     )
-    for row in range(columns // 2):
+    early, middle = 3 * columns // 8, 6 * columns // 8
+    for row in range(early):
         backward(row)
 
     core_copy.wait()
@@ -392,9 +413,26 @@
             )
         )
     plane_all[my_plane] = plane_send[my_plane]
-    for row in range(columns // 2, columns):
+    for row in range(early, middle):
         backward(row)
 
+    for copy in plane_copies:
+        copy.wait()
+    line_send[...] = ordered_sum(plane_all, n_plane)
+    line_copies = [
+        remote(
+            line_send,
+            line_all.at[level],
+            line_send_sems.at[d],
+            line_recv_sems.at[d],
+            line_peer(d),
+        )
+        for d in range(1, n_line)
+    ]
+    line_all[level] = line_send[...]
+
+    for row in range(middle, columns):
+        backward(row)
     top = lax.broadcasted_iota(jnp.int32, (8, hidden), 0)
     mixed = jnp.where(
         top == channels + 1, totals[hidden : hidden + 8], totals_in[0:8] + totals_in[8:16]
@@ -411,34 +449,22 @@
         other_core,
     )
 
-    for copy in plane_copies:
-        copy.wait()
-    line_send[...] = ordered_sum(plane_all, n_plane)
-    line_copies = [
-        remote(
-            line_send,
-            line_all.at[level],
-            line_send_sems.at[d],
-            line_recv_sems.at[d],
-            line_peer(d),
-        )
-        for d in range(1, n_line)
-    ]
-    line_all[level] = line_send[...]
-
-    ext_core_copy.wait()
-    ext_plane_send[...] = ext_core_send[core] + ext_core_recv[...]
-    ext_plane_copies = [
-        remote(
-            ext_plane_send,
-            ext_plane_all.at[my_plane],
-            ext_plane_send_sems.at[d],
-            ext_plane_recv_sems.at[d],
-            plane_peer(d)[1],
-        )
-        for d in range(1, n_plane)
-    ]
-    ext_plane_all[my_plane] = ext_plane_send[...]
+    ext_plane_copies = []
+
+    def start_ext_plane():
+        ext_core_copy.wait()
+        ext_plane_send[...] = ext_core_send[core] + ext_core_recv[...]
+        ext_plane_copies.extend(
+            remote(
+                ext_plane_send,
+                ext_plane_all.at[my_plane],
+                ext_plane_send_sems.at[d],
+                ext_plane_recv_sems.at[d],
+                plane_peer(d)[1],
+            )
+            for d in range(1, n_plane)
+        )
+        ext_plane_all[my_plane] = ext_plane_send[...]
 
     for copy in halo_copies:
         copy.wait()
@@ -466,6 +492,8 @@
             bottom = jnp.where(here, -2.0 * tags_ref[0, i, k].astype(F32), bottom)
             ceiling = jnp.where(here, -2.0 * tags_ref[1, i, k].astype(F32), ceiling)
     for c in range(channels):
+        if c == channels // 2:
+            start_ext_plane()
         own = adj_rows[c]
         low_y = jnp.where(spot_j == 0, bottom * own, pltpu.roll(own, 52, 1) - own)
         up_y = jnp.where(
@@ -538,6 +566,11 @@
     ]
     pair_copies = [to_pair(my_plane, 0)]
     store_part(core, my_plane)
+    for d in range(1, n_plane):
+        spread_copies[d - 1].wait_recv()
+        slot = lax.rem(my_plane + n_plane - d, n_plane)
+        pair_copies.append(to_pair(slot, d))
+        store_part(core, slot)
     for copy in ext_line_copies:
         copy.wait()
     gathered_ext[core] = factor * ordered_sum(ext_line_all, n_line)
@@ -548,11 +581,6 @@
         pair_recv_sems.at[n_plane],
         other_core,
     )
-    for d in range(1, n_plane):
-        spread_copies[d - 1].wait_recv()
-        slot = lax.rem(my_plane + n_plane - d, n_plane)
-        pair_copies.append(to_pair(slot, d))
-        store_part(core, slot)
     ext_pair_copy.wait()
     for h in range(2):
         lanes = slice(h * half, (h + 1) * half)
@@ -660,11 +688,14 @@
             pltpu.VMEM((columns, hidden + 32, line), BF16),
             pltpu.VMEM((columns, hidden, line), F32),
             pltpu.VMEM((columns, hidden, line), BF16),
+            pltpu.VMEM((columns, hidden, line), BF16),
             pltpu.VMEM((hidden + 32, hidden), F32),
             pltpu.VMEM((32, hidden), F32),
             pltpu.VMEM((16, hidden), F32),
             pltpu.VMEM((1, 128), F32),
-            pltpu.VMEM((gx * gz, 1, 128), F32),
+            pltpu.VMEM((2 * n_plane, 1, 128), F32),
+            pltpu.VMEM((1, 128), F32),
+            pltpu.VMEM((n_line, 1, 128), F32),
             pltpu.VMEM((2, hidden, half), F32),
             pltpu.VMEM((hidden, half), F32),
             pltpu.VMEM((n_plane, part, half), F32),
@@ -679,6 +710,7 @@
             pltpu.VMEM((n_line, 16, half), F32),
             dma((11,)),
             dma((2 * n_plane + 5,)),
+            dma((2,)),
             dma((2,)),
             dma((4,)),
             dma((4,)),

time: 33 us -> 34.4 us (1.042)
  Pallas kernels: 32.1 us -> 33.6 us
    pallas_call x1, Pallas kernels: 30.3 us -> 31.8 us  [per_device(): pl.pallas_call(functools.partial(kernel, dims), out_shape=out_shape, in_s...]
where the time goes in v4:
time: 34.4 us; the launch traced here: 34.2 us
  Pallas kernels  33.6 us (98%)
  between operations  0.64 us (2%)
    pallas_call x1, Pallas kernels, per_device(): pl.pallas_call(functools.partial(kernel, dims), out_shape=out_shape, in_s...  31.8 us
    pallas_call x1, Pallas kernels, per_device(): pl.pallas_call(writer, out_shape=out_shape, in_specs=[hbm] * 6, out_specs...  1.83 us

profile of v4, /device:TPU:0, one launch (start us, length us, event | category | flops | bytes accessed | tf_op | source)
XLA Modules:
  0.0 34.2 jit_solution(5273999240206420528)
XLA Ops:
  0.6 31.8 %shard_map.136 = (f32[5,2,4,512]{3,2,1,0:T(4,128)}, f32[5,256]{1,0:T(8,128)}, f32[1,256]{1,0:T(1,128)}, f32[256,256]{1,0:T(8,128)}, f32[1,256]{1,0:T(1,128)}, /*index=5*/f32[5,256]{1,0:T(8,128)}) custom-call(f32[5,2,4,512]{3,2,1,0:T(4,128)} %state_hbm.1, f32[5,2,4,512]{3,2,1,0:T(4,128)} %cot_hbm.1, f32[64,2,4,512]{3,2,1,0:T(4,128)} %inv_hbm.1, ...), custom_call_target="tpu_custom_call" | custom-call | tf_op jit(solution)/shard_map/pallas_call | solution.py:649
  32.4 1.8 %shard_map.137 = (f32[5,2,4,512]{3,2,1,0:T(4,128)}, f32[5,256]{1,0:T(8,128)}, f32[1,256]{1,0:T(1,128)}, f32[256,256]{1,0:T(8,128)}, f32[1,256]{1,0:T(1,128)}, /*index=5*/f32[5,256]{1,0:T(8,128)}) custom-call(f32[5,2,4,512]{3,2,1,0:T(4,128)} %get-tuple-element.18.refs_0_, f32[5,256]{1,0:T(8,128)} %get-tuple-element.19.refs_1_, ...), custom_call_target="tpu_custom_call" | custom-call | tf_op jit(solution)/shard_map/pallas_call | solution.py:736

commit v5 on v3

--- a/solution.py
+++ b/solution.py
@@ -52,8 +52,6 @@
     gbin_ref,
     gbmid_ref,
     gout_ref,
-    gathered,
-    gathered_ext,
     state_ref,
     cot_ref,
     inv_ref,
@@ -81,22 +79,19 @@
     w_out_half,
     bias_mid,
     joints,
-    slopes,
+    bends,
+    hiddens,
     deltas,
     totals,
     totals_in,
     totals_out,
     norm_mine,
     norm_all,
-    core_send,
-    core_recv,
-    plane_send,
     plane_all,
     line_send,
     line_all,
-    ext_core_send,
-    ext_core_recv,
-    ext_plane_send,
+    result,
+    ext_send,
     ext_plane_all,
     ext_line_send,
     ext_line_all,
@@ -105,37 +100,32 @@
     norm_sems,
     halo_send_sems,
     halo_recv_sems,
-    core_sems,
     plane_send_sems,
     plane_recv_sems,
     line_send_sems,
     line_recv_sems,
-    ext_core_sems,
     ext_plane_send_sems,
     ext_plane_recv_sems,
     ext_line_send_sems,
     ext_line_recv_sems,
     spread_send_sems,
     spread_recv_sems,
-    pair_send_sems,
-    pair_recv_sems,
 ):
     gx, gz = dims
     channels, x_elems, z_elems, line = state_ref.shape
     hidden = w_mid_ref.shape[0]
     columns = x_elems * z_elems
     count = gx * gz
-    half = hidden // 2
-    n_plane, n_line = gx * 2, gz // 4
+    n_plane, n_line = gx * 4, gz // 4
     part = hidden // n_plane
+    halves, _, span, _ = plane_all.shape
     nodes = inv_ref.shape[0]
     pieces = 4
     piece = nodes // pieces
     my_x, my_z = lax.axis_index("gx"), lax.axis_index("gz")
     me = my_x * gz + my_z
-    core, side, level = my_z % 2, (my_z // 2) % 2, my_z // 4
-    my_plane = my_x * 2 + side
-    other_core = (my_x, my_z + 1 - 2 * core)
+    spot_z, level = my_z % 4, my_z // 4
+    mine = my_x * 4 + spot_z
 
     loads = [
         pltpu.make_async_copy(src, dst, load_sems.at[spot])
@@ -172,6 +162,30 @@
         return carry
 
     lax.fori_loop(1, count, greet, 0)
+
+    loads[0].wait()
+    squares = state_ref[...] * state_ref[...]
+    squares = jnp.sum(jnp.sum(squares, axis=0), axis=0)
+    folded = squares[:, :128]
+    for start in range(128, line, 128):
+        folded = folded + squares[:, start : start + 128]
+    norm_mine[...] = jnp.sum(folded, axis=0, keepdims=True)
+
+    pl.semaphore_wait(barrier, count - 1)
+
+    def send_norm(step, carry):
+        to = lax.rem(me + step, count)
+        pltpu.make_async_remote_copy(
+            src_ref=norm_mine,
+            dst_ref=norm_all.at[step - 1],
+            send_sem=norm_sems.at[0],
+            recv_sem=norm_sems.at[1],
+            device_id=(to // gz, lax.rem(to, gz)),
+            device_id_type=MESH,
+        ).start()
+        return carry
+
+    lax.fori_loop(1, count, send_norm, 0)
 
     for load in loads[2:]:
         load.wait()
@@ -201,30 +215,6 @@
     totals_in[...] = jnp.zeros_like(totals_in)
     totals_out[...] = jnp.zeros_like(totals_out)
 
-    loads[0].wait()
-    squares = state_ref[...] * state_ref[...]
-    squares = jnp.sum(jnp.sum(squares, axis=0), axis=0)
-    folded = squares[:, :128]
-    for start in range(128, line, 128):
-        folded = folded + squares[:, start : start + 128]
-    norm_mine[...] = jnp.sum(folded, axis=0, keepdims=True)
-
-    pl.semaphore_wait(barrier, count - 1)
-
-    def send_norm(step, carry):
-        to = lax.rem(me + step, count)
-        pltpu.make_async_remote_copy(
-            src_ref=norm_mine,
-            dst_ref=norm_all.at[step - 1],
-            send_sem=norm_sems.at[0],
-            recv_sem=norm_sems.at[1],
-            device_id=(to // gz, lax.rem(to, gz)),
-            device_id_type=MESH,
-        ).start()
-        return carry
-
-    lax.fori_loop(1, count, send_norm, 0)
-
     loads[1].wait()
     for c in range(channels):
         for i in range(x_elems):
@@ -310,7 +300,7 @@
         bend = jnp.tanh(pre)
         gate = 1.0 + bend
         act = pre * gate
-        slopes[row] = gate + act * (1.0 - bend)
+        bends[row] = bend
         joints[row, :hidden, :] = act.astype(BF16)
 
     def second_layer(row):
@@ -321,7 +311,7 @@
         act = pre * gate
         slope_two = gate + act * (1.0 - bend)
         out_grad = grad_rows[row].astype(BF16)
-        totals_out[...] += nt_dot(out_grad, act.astype(BF16))
+        hiddens[row] = act.astype(BF16)
         back_two = nn_dot(w_out_half[...], out_grad)
         deltas[row] = (back_two * slope_two).astype(BF16)
 
@@ -337,20 +327,16 @@
             last_layer(step - 2)
 
     def backward(row):
-        delta_one = nn_dot(w_mid_half[...], deltas[row]) * slopes[row]
+        bend = bends[row]
+        slope = 1.0 + bend + joints[row, :hidden, :].astype(F32) * (1.0 - bend)
+        delta_one = nn_dot(w_mid_half[...], deltas[row]) * slope
         delta_one = delta_one.astype(BF16)
         totals_in[...] += nt_dot(joints[row, hidden:, :], delta_one)
+        totals_out[...] += nt_dot(grad_rows[row].astype(BF16), hiddens[row])
         back = nn_dot(w_back[...], delta_one)
         back = back[:8] + back[8:]
         for c in range(channels):
             back_rows[c, row : row + 1, :] = back[c : c + 1, :]
-
-    def plane_peer(d):
-        to = lax.rem(my_plane + d, n_plane)
-        return to, (to // 2, level * 4 + lax.rem(to, 2) * 2 + core)
-
-    def line_peer(d):
-        return (my_x, lax.rem(level + d, n_line) * 4 + side * 2 + core)
 
     def remote(src, dst, send_sem, recv_sem, to):
         copy = pltpu.make_async_remote_copy(
@@ -364,81 +350,101 @@
         copy.start()
         return copy
 
+    def plane_peer(d):
+        to = lax.rem(mine + d, n_plane)
+        return to, (to // 4, level * 4 + lax.rem(to, 4))
+
+    def line_peer(d):
+        return (my_x, lax.rem(level + d, n_line) * 4 + spot_z)
+
     def ordered_sum(ref, size):
         return sum((ref[q] for q in range(1, size)), ref[0])
 
-    for h in range(2):
-        core_send[h] = totals[0:hidden, h * half : (h + 1) * half]
-    core_copy = remote(
-        core_send.at[1 - core], core_recv, core_sems.at[0], core_sems.at[1], other_core
-    )
-    for row in range(columns // 2):
+    def wait_all(copies):
+        for copy in copies:
+            copy.wait()
+
+    def block_of(owner, t):
+        return pl.ds(pl.multiple_of(owner * part + t * span, span), span)
+
+    plane_copies = []
+    for t in range(halves):
+        copies = []
+        for d in range(1, n_plane):
+            to, device = plane_peer(d)
+            copies.append(
+                remote(
+                    totals.at[block_of(to, t)],
+                    plane_all.at[t, mine],
+                    plane_send_sems.at[t, d],
+                    plane_recv_sems.at[t, d],
+                    device,
+                )
+            )
+        plane_copies.append(copies)
+        plane_all[t, mine] = totals[block_of(mine, t), :]
+
+    line_copies = []
+
+    def start_line(t):
+        wait_all(plane_copies[t])
+        line_send[t] = ordered_sum(plane_all.at[t], n_plane)
+        line_copies.append(
+            [
+                remote(
+                    line_send.at[t],
+                    line_all.at[t, level],
+                    line_send_sems.at[t, d],
+                    line_recv_sems.at[t, d],
+                    line_peer(d),
+                )
+                for d in range(1, n_line)
+            ]
+        )
+        line_all[t, level] = line_send[t]
+
+    early = 5 * columns // 8
+    for row in range(early):
         backward(row)
-
-    core_copy.wait()
-    for q in range(n_plane):
-        rows = slice(q * part, (q + 1) * part)
-        plane_send[q] = core_send[core, rows, :] + core_recv[rows, :]
-    plane_copies = []
-    for d in range(1, n_plane):
-        to, device = plane_peer(d)
-        plane_copies.append(
-            remote(
-                plane_send.at[to],
-                plane_all.at[my_plane],
-                plane_send_sems.at[d],
-                plane_recv_sems.at[d],
-                device,
-            )
-        )
-    plane_all[my_plane] = plane_send[my_plane]
-    for row in range(columns // 2, columns):
+    start_line(0)
+    for row in range(early, columns):
         backward(row)
 
     top = lax.broadcasted_iota(jnp.int32, (8, hidden), 0)
-    mixed = jnp.where(
+    ext_send[0:8, :] = jnp.where(
         top == channels + 1, totals[hidden : hidden + 8], totals_in[0:8] + totals_in[8:16]
     )
-    for h in range(2):
-        lanes = slice(h * half, (h + 1) * half)
-        ext_core_send[h, 0:8, :] = mixed[:, lanes]
-        ext_core_send[h, 8:16, :] = totals_out[0:8, lanes]
-    ext_core_copy = remote(
-        ext_core_send.at[1 - core],
-        ext_core_recv,
-        ext_core_sems.at[0],
-        ext_core_sems.at[1],
-        other_core,
-    )
-
-    for copy in plane_copies:
-        copy.wait()
-    line_send[...] = ordered_sum(plane_all, n_plane)
-    line_copies = [
-        remote(
-            line_send,
-            line_all.at[level],
-            line_send_sems.at[d],
-            line_recv_sems.at[d],
-            line_peer(d),
-        )
-        for d in range(1, n_line)
-    ]
-    line_all[level] = line_send[...]
-
-    ext_core_copy.wait()
-    ext_plane_send[...] = ext_core_send[core] + ext_core_recv[...]
+    ext_send[8:16, :] = totals_out[0:8]
     ext_plane_copies = [
         remote(
-            ext_plane_send,
-            ext_plane_all.at[my_plane],
+            ext_send,
+            ext_plane_all.at[mine],
             ext_plane_send_sems.at[d],
             ext_plane_recv_sems.at[d],
             plane_peer(d)[1],
         )
         for d in range(1, n_plane)
     ]
-    ext_plane_all[my_plane] = ext_plane_send[...]
+    ext_plane_all[mine] = ext_send[...]
+    for t in range(1, halves):
+        start_line(t)
+
+    ext_line_copies = []
+
+    def start_ext_line():
+        wait_all(ext_plane_copies)
+        ext_line_send[...] = ordered_sum(ext_plane_all, n_plane)
+        ext_line_copies.extend(
+            remote(
+                ext_line_send,
+                ext_line_all.at[level],
+                ext_line_send_sems.at[d],
+                ext_line_recv_sems.at[d],
+                line_peer(d),
+            )
+            for d in range(1, n_line)
+        )
+        ext_line_all[level] = ext_line_send[...]
 
     for copy in halo_copies:
         copy.wait()
@@ -466,6 +472,8 @@
             bottom = jnp.where(here, -2.0 * tags_ref[0, i, k].astype(F32), bottom)
             ceiling = jnp.where(here, -2.0 * tags_ref[1, i, k].astype(F32), ceiling)
     for c in range(channels):
+        if c == channels // 2:
+            start_ext_line()
         own = adj_rows[c]
         low_y = jnp.where(spot_j == 0, bottom * own, pltpu.roll(own, 52, 1) - own)
         up_y = jnp.where(
@@ -489,88 +497,36 @@
         copy.start()
         stores.append(copy)
 
-    def store_part(h, q):
-        dst = gmid_hbm.at[
-            pl.ds(pl.multiple_of(q * part, part), part),
-            pl.ds(pl.multiple_of(h * half, half), half),
-        ]
-        store(gathered.at[h, q], dst)
-
     store(gstate_ref, gstate_hbm)
 
-    for copy in ext_plane_copies:
-        copy.wait()
-    ext_line_send[...] = ordered_sum(ext_plane_all, n_plane)
-    ext_line_copies = [
-        remote(
-            ext_line_send,
-            ext_line_all.at[level],
-            ext_line_send_sems.at[d],
-            ext_line_recv_sems.at[d],
-            line_peer(d),
-        )
-        for d in range(1, n_line)
-    ]
-    ext_line_all[level] = ext_line_send[...]
-
-    def to_pair(slot, d):
-        return remote(
-            gathered.at[core, slot],
-            gathered.at[core, slot],
-            pair_send_sems.at[d],
-            pair_recv_sems.at[d],
-            other_core,
-        )
-
     factor = 4.0 / math.sqrt(entry_count // channels)
-    for copy in line_copies:
-        copy.wait()
-    gathered[core, my_plane] = factor * ordered_sum(line_all, n_line)
-    spread_copies = [
-        remote(
-            gathered.at[core, my_plane],
-            gathered.at[core, my_plane],
-            spread_send_sems.at[d],
-            spread_recv_sems.at[d],
-            plane_peer(d)[1],
-        )
-        for d in range(1, n_plane)
-    ]
-    pair_copies = [to_pair(my_plane, 0)]
-    store_part(core, my_plane)
-    for copy in ext_line_copies:
-        copy.wait()
-    gathered_ext[core] = factor * ordered_sum(ext_line_all, n_line)
-    ext_pair_copy = remote(
-        gathered_ext.at[core],
-        gathered_ext.at[core],
-        pair_send_sems.at[n_plane],
-        pair_recv_sems.at[n_plane],
-        other_core,
-    )
-    for d in range(1, n_plane):
-        spread_copies[d - 1].wait_recv()
-        slot = lax.rem(my_plane + n_plane - d, n_plane)
-        pair_copies.append(to_pair(slot, d))
-        store_part(core, slot)
-    ext_pair_copy.wait()
-    for h in range(2):
-        lanes = slice(h * half, (h + 1) * half)
-        gin_ref[:, lanes] = gathered_ext[h, 0:channels]
-        gbin_ref[:, lanes] = gathered_ext[h, channels : channels + 1]
-        gbmid_ref[:, lanes] = gathered_ext[h, channels + 1 : channels + 2]
-        gout_ref[:, lanes] = gathered_ext[h, 8 : 8 + channels]
+    spread_copies = []
+    for t in range(halves):
+        wait_all(line_copies[t])
+        result[t] = factor * ordered_sum(line_all.at[t], n_line)
+        for d in range(1, n_plane):
+            spread_copies.append(
+                remote(
+                    result.at[t],
+                    gmid_hbm.at[block_of(mine, t)],
+                    spread_send_sems.at[t, d],
+                    spread_recv_sems.at[t, d],
+                    plane_peer(d)[1],
+                )
+            )
+        store(result.at[t], gmid_hbm.at[block_of(mine, t)])
+    wait_all(ext_line_copies)
+    small = factor * ordered_sum(ext_line_all, n_line)
+    gin_ref[...] = small[0:channels]
+    gbin_ref[...] = small[channels : channels + 1]
+    gbmid_ref[...] = small[channels + 1 : channels + 2]
+    gout_ref[...] = small[8 : 8 + channels]
     store(gin_ref, gin_hbm)
     store(gbin_ref, gbin_hbm)
     store(gbmid_ref, gbmid_hbm)
     store(gout_ref, gout_hbm)
-    for d in range(n_plane):
-        pair_copies[d].wait()
-        store_part(1 - core, lax.rem(my_plane + n_plane - d, n_plane))
-    for copy in spread_copies:
-        copy.wait_send()
-    for copy in stores:
-        copy.wait()
+    wait_all(spread_copies)
+    wait_all(stores)
 
 
 def writer(*refs):
@@ -598,9 +554,10 @@
     channels, x_elems, z_elems, line = state.shape
     hidden = w_mid.shape[0]
     columns = x_elems * z_elems
-    n_plane, n_line = gx * 2, gz // 4
+    n_plane, n_line = gx * 4, gz // 4
     part = hidden // n_plane
-    half = hidden // 2
+    halves = 2 if part % 16 == 0 else 1
+    span = part // halves
     vmem = pl.BlockSpec(memory_space=pltpu.VMEM)
     hbm = pl.BlockSpec(memory_space=pltpu.HBM)
     rows = pltpu.VMEM((channels, columns, line), F32)
@@ -629,8 +586,6 @@
             pltpu.VMEM((1, hidden), F32),
             pltpu.VMEM((1, hidden), F32),
             pltpu.VMEM((channels, hidden), F32),
-            pltpu.VMEM((2, n_plane, part, half), F32),
-            pltpu.VMEM((2, 16, half), F32),
             same(state),
             same(cotangent),
             same(local_inverse),
@@ -660,42 +615,35 @@
             pltpu.VMEM((columns, hidden + 32, line), BF16),
             pltpu.VMEM((columns, hidden, line), F32),
             pltpu.VMEM((columns, hidden, line), BF16),
+            pltpu.VMEM((columns, hidden, line), BF16),
             pltpu.VMEM((hidden + 32, hidden), F32),
             pltpu.VMEM((32, hidden), F32),
             pltpu.VMEM((16, hidden), F32),
             pltpu.VMEM((1, 128), F32),
             pltpu.VMEM((gx * gz, 1, 128), F32),
-            pltpu.VMEM((2, hidden, half), F32),
-            pltpu.VMEM((hidden, half), F32),
-            pltpu.VMEM((n_plane, part, half), F32),
-            pltpu.VMEM((n_plane, part, half), F32),
-            pltpu.VMEM((part, half), F32),
-            pltpu.VMEM((n_line, part, half), F32),
-            pltpu.VMEM((2, 16, half), F32),
-            pltpu.VMEM((16, half), F32),
-            pltpu.VMEM((16, half), F32),
-            pltpu.VMEM((n_plane, 16, half), F32),
-            pltpu.VMEM((16, half), F32),
-            pltpu.VMEM((n_line, 16, half), F32),
+            pltpu.VMEM((halves, n_plane, span, hidden), F32),
+            pltpu.VMEM((halves, span, hidden), F32),
+            pltpu.VMEM((halves, n_line, span, hidden), F32),
+            pltpu.VMEM((halves, span, hidden), F32),
+            pltpu.VMEM((16, hidden), F32),
+            pltpu.VMEM((n_plane, 16, hidden), F32),
+            pltpu.VMEM((16, hidden), F32),
+            pltpu.VMEM((n_line, 16, hidden), F32),
             dma((11,)),
-            dma((2 * n_plane + 5,)),
+            dma((halves + 5,)),
             dma((2,)),
             dma((4,)),
             dma((4,)),
-            dma((2,)),
+            dma((halves, n_plane)),
+            dma((halves, n_plane)),
+            dma((halves, n_line)),
+            dma((halves, n_line)),
             dma((n_plane,)),
             dma((n_plane,)),
             dma((n_line,)),
             dma((n_line,)),
-            dma((2,)),
-            dma((n_plane,)),
-            dma((n_plane,)),
-            dma((n_line,)),
-            dma((n_line,)),
-            dma((n_plane,)),
-            dma((n_plane,)),
-            dma((n_plane + 1,)),
-            dma((n_plane + 1,)),
+            dma((halves, n_plane)),
+            dma((halves, n_plane)),
         ],
         compiler_params=pltpu.CompilerParams(
             collective_id=0, has_side_effects=True, vmem_limit_bytes=62 * 1024 * 1024

time: 33 us -> 31.4 us (0.952)
  Pallas kernels: 32.1 us -> 30.6 us
    pallas_call x1, Pallas kernels: 30.3 us -> 28.8 us  [per_device(): pl.pallas_call(functools.partial(kernel, dims), out_shape=out_shape, in_s...]
where the time goes in v5:
time: 31.4 us; the launch traced here: 31.2 us
  Pallas kernels  30.6 us (97%)
  between operations  0.64 us (2%)
    pallas_call x1, Pallas kernels, per_device(): pl.pallas_call(functools.partial(kernel, dims), out_shape=out_shape, in_s...  28.8 us
    pallas_call x1, Pallas kernels, per_device(): pl.pallas_call(writer, out_shape=out_shape, in_specs=[hbm] * 6, out_specs...  1.83 us

profile of v5, /device:TPU:0, one launch (start us, length us, event | category | flops | bytes accessed | tf_op | source)
XLA Modules:
  0.0 31.2 jit_solution(12016140782261738844)
XLA Ops:
  0.6 28.8 %shard_map.136 = (f32[5,2,4,512]{3,2,1,0:T(4,128)}, f32[5,256]{1,0:T(8,128)}, f32[1,256]{1,0:T(1,128)}, f32[256,256]{1,0:T(8,128)}, f32[1,256]{1,0:T(1,128)}, /*index=5*/f32[5,256]{1,0:T(8,128)}) custom-call(f32[5,2,4,512]{3,2,1,0:T(4,128)} %state_hbm.1, f32[5,2,4,512]{3,2,1,0:T(4,128)} %cot_hbm.1, f32[64,2,4,512]{3,2,1,0:T(4,128)} %inv_hbm.1, ...), custom_call_target="tpu_custom_call" | custom-call | tf_op jit(solution)/shard_map/pallas_call | solution.py:578
  29.4 1.8 %shard_map.137 = (f32[5,2,4,512]{3,2,1,0:T(4,128)}, f32[5,256]{1,0:T(8,128)}, f32[1,256]{1,0:T(1,128)}, f32[256,256]{1,0:T(8,128)}, f32[1,256]{1,0:T(1,128)}, /*index=5*/f32[5,256]{1,0:T(8,128)}) custom-call(f32[5,2,4,512]{3,2,1,0:T(4,128)} %get-tuple-element.18.refs_0_, f32[5,256]{1,0:T(8,128)} %get-tuple-element.19.refs_1_, ...), custom_call_target="tpu_custom_call" | custom-call | tf_op jit(solution)/shard_map/pallas_call | solution.py:652

commit v6 on v5

--- a/solution.py
+++ b/solution.py
@@ -41,15 +41,10 @@
     w_mid_hbm,
     b_mid_hbm,
     w_out_ref,
-    gstate_hbm,
-    gin_hbm,
-    gbin_hbm,
-    gmid_hbm,
-    gbmid_hbm,
-    gout_hbm,
     gstate_ref,
     gin_ref,
     gbin_ref,
+    gmid_ref,
     gbmid_ref,
     gout_ref,
     state_ref,
@@ -96,7 +91,6 @@
     ext_line_send,
     ext_line_all,
     load_sems,
-    store_sems,
     norm_sems,
     halo_send_sems,
     halo_recv_sems,
@@ -490,15 +484,6 @@
         back_rows[c] = own + 0.5 * KAPPA * jump + inv_norm * back_rows[c]
         for i in range(x_elems):
             gstate_ref[c, i] = back_rows[c, i * z_elems : (i + 1) * z_elems, :]
-    stores = []
-
-    def store(src, dst):
-        copy = pltpu.make_async_copy(src, dst, store_sems.at[len(stores)])
-        copy.start()
-        stores.append(copy)
-
-    store(gstate_ref, gstate_hbm)
-
     factor = 4.0 / math.sqrt(entry_count // channels)
     spread_copies = []
     for t in range(halves):
@@ -508,45 +493,32 @@
             spread_copies.append(
                 remote(
                     result.at[t],
-                    gmid_hbm.at[block_of(mine, t)],
+                    gmid_ref.at[block_of(mine, t)],
                     spread_send_sems.at[t, d],
                     spread_recv_sems.at[t, d],
                     plane_peer(d)[1],
                 )
             )
-        store(result.at[t], gmid_hbm.at[block_of(mine, t)])
+        gmid_ref[block_of(mine, t), :] = result[t]
     wait_all(ext_line_copies)
     small = factor * ordered_sum(ext_line_all, n_line)
     gin_ref[...] = small[0:channels]
     gbin_ref[...] = small[channels : channels + 1]
     gbmid_ref[...] = small[channels + 1 : channels + 2]
     gout_ref[...] = small[8 : 8 + channels]
-    store(gin_ref, gin_hbm)
-    store(gbin_ref, gbin_hbm)
-    store(gbmid_ref, gbmid_hbm)
-    store(gout_ref, gout_hbm)
     wait_all(spread_copies)
-    wait_all(stores)
 
 
 def writer(*refs):
-    size = (len(refs) - 1) // 3
-    sems = refs[-1]
-    sources, results, held = refs[:size], refs[size : 2 * size], refs[2 * size : -1]
-    loads = [
-        pltpu.make_async_copy(sources[spot], held[spot], sems.at[spot]) for spot in range(size)
-    ]
-    stores = [
-        pltpu.make_async_copy(held[spot], results[spot], sems.at[size + spot])
+    size = len(refs) // 2
+    copies = [
+        pltpu.make_async_copy(refs[spot], refs[size + spot], refs[-1].at[spot])
         for spot in range(size)
     ]
-    for load in loads:
-        load.start()
-    for load, store in zip(loads, stores):
-        load.wait()
-        store.start()
-    for store in stores:
-        store.wait()
+    for copy in copies:
+        copy.start()
+    for copy in copies:
+        copy.wait()
 
 
 def per_device(dims, state, cotangent, local_inverse, wall_tags, w_in, b_in, w_mid, b_mid, w_out):
@@ -577,15 +549,10 @@
     )
     out = pl.pallas_call(
         functools.partial(kernel, dims),
-        out_shape=out_shape,
+        out_shape=tuple(pltpu.VMEM(o.shape, F32) for o in out_shape),
         in_specs=[hbm] * 8 + [vmem],
-        out_specs=(hbm,) * 6,
+        out_specs=(vmem,) * 6,
         scratch_shapes=[
-            same(state),
-            pltpu.VMEM((channels, hidden), F32),
-            pltpu.VMEM((1, hidden), F32),
-            pltpu.VMEM((1, hidden), F32),
-            pltpu.VMEM((channels, hidden), F32),
             same(state),
             same(cotangent),
             same(local_inverse),
@@ -630,7 +597,6 @@
             pltpu.VMEM((16, hidden), F32),
             pltpu.VMEM((n_line, 16, hidden), F32),
             dma((11,)),
-            dma((halves + 5,)),
             dma((2,)),
             dma((4,)),
             dma((4,)),
@@ -651,11 +617,11 @@
     )(state, cotangent, local_inverse, wall_tags, w_in, b_in, w_mid, b_mid, w_out.T)
     out = pl.pallas_call(
         writer,
-        out_shape=out_shape,
-        in_specs=[hbm] * 6,
+        out_shape=tuple(pltpu.HBM(o.shape, F32) for o in out_shape),
+        in_specs=[vmem] * 6,
         out_specs=(hbm,) * 6,
-        scratch_shapes=[pltpu.VMEM(o.shape, F32) for o in out_shape] + [dma((12,))],
-        compiler_params=pltpu.CompilerParams(vmem_limit_bytes=62 * 1024 * 1024),
+        scratch_shapes=[dma((6,))],
+        compiler_params=pltpu.CompilerParams(vmem_limit_bytes=8 * 1024 * 1024),
     )(*out)
     return out[0], out[1], out[2].reshape(hidden), out[3], out[4].reshape(hidden), out[5].T
 

time: 31.4 us -> 29.9 us (0.952)
  Pallas kernels: 30.6 us -> 29.1 us
    pallas_call x2, Pallas kernels: 30.6 us -> 29.1 us  [the longest x1 28.3 us: per_device(): pl.pallas_call(functools.partial(kernel, dims), out_shape=tuple((pltpu.VM...]
where the time goes in v6:
time: 29.9 us; the launch traced here: 29.7 us
  Pallas kernels  29.1 us (97%)
  between operations  0.64 us (2%)
    pallas_call x1, Pallas kernels, per_device(): pl.pallas_call(functools.partial(kernel, dims), out_shape=tuple((pltpu.VM...  28.3 us
    pallas_call x1, Pallas kernels, per_device(): pl.pallas_call(writer, out_shape=tuple((pltpu.HBM(o.shape, F32) for o in...  0.8 us

profile of v6, /device:TPU:0, one launch (start us, length us, event | category | flops | bytes accessed | tf_op | source)
XLA Modules:
  0.0 29.7 jit_solution(10943820333998223155)
XLA Ops:
  0.6 28.3 %shard_map.136 = (f32[5,2,4,512]{3,2,1,0:T(4,128)S(1)}, f32[5,256]{1,0:T(8,128)S(1)}, f32[1,256]{1,0:T(1,128)S(1)}, f32[256,256]{1,0:T(8,128)S(1)}, f32[1,256]{1,0:T(1,128)S(1)}, /*index=5*/f32[5,256]{1,0:T(8,128)S(1)}) custom-call(f32[5,2,4,512]{3,2,1,0:T(4,128)} %state_hbm.1, f32[5,2,4,512]{3,2,1,0:T(4,128)} %cot_hbm.1, f32[64,2,4,512]{3,2,1,0:T(4,128)} %inv_hbm.1, ...), custom_call_target="tpu_custom_call" | custom-call | tf_op jit(solution)/shard_map/pallas_call | solution.py:550
  28.9 0.8 %shard_map.137 = (f32[5,2,4,512]{3,2,1,0:T(4,128)}, f32[5,256]{1,0:T(8,128)}, f32[1,256]{1,0:T(1,128)}, f32[256,256]{1,0:T(8,128)}, f32[1,256]{1,0:T(1,128)}, /*index=5*/f32[5,256]{1,0:T(8,128)}) custom-call(f32[5,2,4,512]{3,2,1,0:T(4,128)S(1)} %get-tuple-element.18.refs_0_, f32[5,256]{1,0:T(8,128)S(1)} %get-tuple-element.19.refs_1_, ...), custom_call_target="tpu_custom_call" | custom-call | tf_op jit(solution)/shard_map/pallas_call | solution.py:618
